TPU v7x, 256 devices: a whole 4x4x8 slice. The times are simulated.
256 devices in a mesh: ctx: 128 (over x, y_lo, z, core), tp: 2 (over y_hi).
Axes of the slice: x: 4, y: 4 (y_hi: 2, y_lo: 2; y = y_hi * 2 + y_lo), z: 8, core: 2. Of those that a mesh axis runs over, the one named last changes fastest.
Arguments:
- query_rows: bfloat16 [16384, 8192], P('ctx', 'tp'), may hold values from -6 to 6
- key_rows: bfloat16 [16384, 8192], P('ctx', 'tp'), may hold values from -6 to 6
- value_rows: bfloat16 [16384, 8192], P('ctx', 'tp'), may hold values from -6 to 6
- decay_rate: float32 [8, 8192], P(None, 'tp'), may hold values from 6.1035157e-06 to 0.05
- residue: float32 [8, 8192], P(None, 'tp'), may hold values from -1.5 to 1.5
- norm_gain: float32 [8192], P('tp'), may hold values from 0.5 to 1.5
- grad_out: bfloat16 [16384, 8192], P('ctx', 'tp'), may hold values from -6 to 6
Outputs:
- normed_out: bfloat16 [16384, 8192], P('ctx', 'tp')
- grad_query: bfloat16 [16384, 8192], P('ctx', 'tp')
- grad_key: bfloat16 [16384, 8192], P('ctx', 'tp')
- grad_value: bfloat16 [16384, 8192], P('ctx', 'tp')
- grad_residue: float32 [8, 8192], P(None, 'tp')
All inputs are finite; a program needn't handle non-finite values.
Results may differ from a plain program's by a relative error of at most 0.0029.
Values sent between devices are 32-bit elements; how exact they have to be, the bound alone decides.
No kernel may reach another device: no remote copies, remote signals or barrier semaphores. Data moves between devices by JAX's collectives and lax.ppermute only.
A program may use at most 192 MiB of HBM per device.

v0:
```python
import jax
import jax.numpy as jnp
from jax import lax
from jax.sharding import PartitionSpec as P

D = 8192


channel_block = 512
norm_eps = 1e-05
exact_mode = lax.Precision.HIGHEST


def carried_in(value, axis, join, neutral, backward):
    count, mine = (lax.axis_size(axis), lax.axis_index(axis))
    pieces = jax.tree.map(lambda part: lax.all_gather(part, axis), value)
    if backward:
        pieces = jax.tree.map(lambda part: part[::-1], pieces)
        mine = count - 1 - mine
    total = jax.tree.map(
        lambda part, zero: jnp.full_like(part, 0) + jnp.asarray(zero, part.dtype), value, neutral
    )

    def turn(position, total):
        longer = join(total, jax.tree.map(lambda part: part[position], pieces))
        return jax.tree.map(lambda new, old: jnp.where(position < mine, new, old), longer, total)

    return lax.fori_loop(0, count - 1, turn, total)


def split_blocks(source, block_count):
    extent = source.shape
    parted = source.reshape(extent[:-1] + (block_count, extent[-1] // block_count))
    return jnp.moveaxis(parted, -2, 0)


def join_blocks(stacked):
    moved_axes = jnp.moveaxis(stacked, 0, -2)
    return moved_axes.reshape(
        moved_axes.shape[:-2] + (moved_axes.shape[-2] * moved_axes.shape[-1],)
    )


def row_powers(decay_part, exponents):
    return jnp.exp(-decay_part[None] * exponents[:, None, None])


def on_device(query_rows, key_rows, value_rows, decay_rate, residue, norm_gain, grad_out):
    row_count = query_rows.shape[0]
    channels = query_rows.shape[1]
    block_width = min(channel_block, channels)
    block_count = channels // block_width
    query_float = query_rows.astype(jnp.float32)
    key_float = key_rows.astype(jnp.float32)
    value_float = value_rows.astype(jnp.float32)
    grad_float = grad_out.astype(jnp.float32)
    product_in = key_float * value_float
    rows_iota = lax.broadcasted_iota(jnp.int32, (row_count, row_count), 0)
    cols_iota = lax.broadcasted_iota(jnp.int32, (row_count, row_count), 1)
    lower_ones = (rows_iota >= cols_iota).astype(jnp.float32)
    upper_ones = (rows_iota <= cols_iota).astype(jnp.float32)
    steps_up = jnp.arange(row_count, dtype=jnp.float32)
    decay_blocks = split_blocks(decay_rate, block_count)
    residue_blocks = split_blocks(residue, block_count)
    product_blocks = split_blocks(product_in, block_count)
    zero_state = jnp.zeros_like(decay_rate)

    def forward_local(pieces):
        product_part, decay_part, residue_part = pieces
        in_scale = jnp.sqrt(-jnp.expm1(-2.0 * decay_part))
        shrink = row_powers(decay_part, steps_up)
        weighted = in_scale[None] * product_part[:, None, :] / shrink
        summed = jnp.dot(lower_ones, weighted.reshape(row_count, -1), precision=exact_mode)
        states_local = shrink * summed.reshape(weighted.shape)
        return (jnp.sum(residue_part[None] * states_local, axis=1), states_local[row_count - 1])

    filtered_local, end_state = lax.map(
        forward_local, (product_blocks, decay_blocks, residue_blocks)
    )
    filtered_local = join_blocks(filtered_local)
    end_state = join_blocks(end_state)

    def chain_decay(previous, following):
        return (previous[0] * following[0], following[0] * previous[1] + following[1])

    whole_decay = jnp.exp(-decay_rate * row_count)
    _, entry_state = carried_in(
        (whole_decay, end_state), "ctx", chain_decay, (jnp.ones_like(end_state), zero_state), False
    )
    entry_blocks = split_blocks(entry_state, block_count)

    def forward_entry(pieces):
        decay_part, residue_part, entry_part = pieces
        shrink = row_powers(decay_part, steps_up)
        return jnp.sum(shrink * (jnp.exp(-decay_part) * residue_part * entry_part)[None], axis=1)

    filtered = filtered_local + join_blocks(
        lax.map(forward_entry, (decay_blocks, residue_blocks, entry_blocks))
    )
    gated = query_float * filtered
    weighted_grad = norm_gain[None, :] * grad_float
    squares, dot_sums = lax.psum(
        (jnp.sum(gated * gated, axis=1), jnp.sum(weighted_grad * gated, axis=1)), "tp"
    )
    rms_scale = jnp.sqrt(squares / D + norm_eps)
    normed_out = (gated * norm_gain[None, :] / rms_scale[:, None]).astype(jnp.bfloat16)
    grad_gated = (
        weighted_grad / rms_scale[:, None] - gated * (dot_sums / (D * rms_scale**3))[:, None]
    )
    grad_query = (grad_gated * filtered).astype(jnp.bfloat16)
    grad_filtered = grad_gated * query_float

    def backward_local(pieces):
        grad_part, product_part, decay_part, residue_part, entry_part = pieces
        in_scale = jnp.sqrt(-jnp.expm1(-2.0 * decay_part))
        shrink = row_powers(decay_part, steps_up)
        reverse_sum = jnp.dot(
            upper_ones,
            (shrink * grad_part[:, None, :]).reshape(row_count, -1),
            precision=exact_mode,
        )
        adjoint_local = reverse_sum.reshape(shrink.shape) / shrink
        leading = adjoint_local[0]
        residue_term = (
            in_scale * jnp.sum(adjoint_local * product_part[:, None, :], axis=0)
            + jnp.exp(-decay_part) * leading * entry_part
        )
        product_term = jnp.sum((in_scale * residue_part)[None] * adjoint_local, axis=1)
        return (residue_term, leading, product_term)

    residue_term, leading, product_term = lax.map(
        backward_local,
        (
            split_blocks(grad_filtered, block_count),
            product_blocks,
            decay_blocks,
            residue_blocks,
            entry_blocks,
        ),
    )
    grad_residue = lax.psum(join_blocks(residue_term), "ctx")
    leading = join_blocks(leading)
    back_decay = jnp.exp(-decay_rate * row_count)
    _, after_state = carried_in(
        (back_decay, leading), "ctx", chain_decay, (jnp.ones_like(leading), zero_state), True
    )

    def backward_entry(pieces):
        decay_part, residue_part, after_part = pieces
        in_scale = jnp.sqrt(-jnp.expm1(-2.0 * decay_part))
        shrink = row_powers(decay_part, steps_up)
        scaled = jnp.exp(-decay_part * row_count) * in_scale * residue_part * after_part
        return jnp.sum(scaled[None] / shrink, axis=1)

    grad_product = join_blocks(product_term) + join_blocks(
        lax.map(
            backward_entry, (decay_blocks, residue_blocks, split_blocks(after_state, block_count))
        )
    )
    grad_key = (grad_product * value_float).astype(jnp.bfloat16)
    grad_value = (grad_product * key_float).astype(jnp.bfloat16)
    return (normed_out, grad_query, grad_key, grad_value, grad_residue)


def solution(mesh):
    return jax.shard_map(
        on_device,
        mesh=mesh,
        in_specs=(
            P("ctx", "tp"),
            P("ctx", "tp"),
            P("ctx", "tp"),
            P(None, "tp"),
            P(None, "tp"),
            P("tp"),
            P("ctx", "tp"),
        ),
        out_specs=(P("ctx", "tp"), P("ctx", "tp"), P("ctx", "tp"), P("ctx", "tp"), P(None, "tp")),
        check_vma=False,
    )
```

profile of v0, /device:TPU:1, one launch (start us, length us, event | category | flops | bytes accessed | tf_op | source)
XLA Modules:
  0.0 2052.6 jit_solution(621177640128863486)
XLA Ops:
  14.6 127.4 %while.82 = (s32[]{:T(128)}, f32[8,128,512]{1,2,0:T(8,128)}, f32[8,8,512]{0,2,1:T(8,128)}, f32[8,8,512]{2,1,0:T(8,128)S(1)}, f32[8,8,512]{2,1,0:T(8,128)S(1)}, /*index=5*/f32[8,128,512]{1,2,0:T(8,128)}, s32[]{:T(128)}, s32[]{:T(128)}) while((s32[]{:T(128)}, f32[8,128,512]{1,2,0:T(8,128)}, f32[8,8,512]{0,2,1:T(8,128)}, ...), condition=%wide.region_2.3_spmd.clone.clone, body=%wide.region_0.2_spmd.clone.clone.sunk | while | flops 808955904 | bytes 17072736 | solution.py:77
  17.7 3.7 fusion.62
  23.4 5.7 dynamic_update_slice.50
  32.9 3.7 fusion.62
  38.7 6.4 dynamic_update_slice.50
  49.0 3.7 fusion.62
  54.7 6.4 dynamic_update_slice.50
  65.0 3.7 fusion.62
  70.7 6.4 dynamic_update_slice.50
  81.0 3.7 fusion.62
  86.7 6.4 dynamic_update_slice.50
  97.0 3.7 fusion.62
  102.7 6.4 dynamic_update_slice.50
  113.0 3.7 fusion.62
  118.8 6.4 dynamic_update_slice.50
  129.0 3.7 fusion.62
  134.8 6.4 dynamic_update_slice.50
  142.0 2.9 copy.69
  145.7 232.2 %all-gather.5.cloned.1.call-done = f32[128,8,4096]{2,1,0:T(8,128)} async-done(((f32[1,8,4096]{2,1,0:T(8,128)}), f32[128,8,4096]{2,1,0:T(8,128)}) %all-gather.5.cloned.1.call-update) | async-done | bytes 16777232 | tf_op jit(solution)/shard_map/all_gather | solution.py:16
  377.9 231.9 %all-gather.9.cloned.1.call-done = f32[1024,4096]{1,0:T(8,128)} async-done(((f32[8,4096]{1,0:T(8,128)}), f32[1024,4096]{1,0:T(8,128)}) %all-gather.9.cloned.1.call-update) | async-done | bytes 16777232 | tf_op jit(solution)/shard_map/all_gather | solution.py:16
  609.9 138.5 %while.84 = (s32[]{:T(128)}, f32[8,4096]{1,0:T(8,128)S(1)}, s32[]{:T(128)}, f32[128,8,4096]{2,1,0:T(8,128)}, f32[128,8,4096]{2,1,0:T(8,128)}, /*index=5*/s32[]{:T(128)}, s32[]{:T(128)}) while((s32[]{:T(128)}, f32[8,4096]{1,0:T(8,128)S(1)}, s32[]{:T(128)}, f32[128,8,4096]{2,1,0:T(8,128)}, f32[128,8,4096]{2,1,0:T(8,128)}, ...), condition=%wide.region_4.5_spmd.clone, body=%wide.region_3.4_spmd.clone.sunk | while | flops 131076 | bytes 524389 | solution.py:28
  749.9 13.5 while.80
  763.4 3.1 add.104
  770.6 5.5 all-reduce
  776.1 4.4 convert_multiply_fusion.3
  780.5 2.9 copy.82
  785.0 90.9 %while.83 = (s32[]{:T(128)}, f32[8,8,512]{2,1,0:T(8,128)S(1)}, f32[8,8,512]{2,1,0:T(8,128)}, f32[8,128,512]{2,1,0:T(8,128)}, f32[8,8,512]{2,1,0:T(8,128)S(1)}, /...) while((s32[]{:T(128)}, f32[8,8,512]{2,1,0:T(8,128)S(1)}, ...), condition=%wide.region_15.16_spmd.clone.clone, body=%wide.region_12.15_spmd.clone.clone.sunk | while | flops 810557440 | bytes 17368172 | solution.py:131
  786.8 3.3 fusion.65
  790.1 2.2 copy.112
  798.1 3.3 fusion.65
  801.4 2.2 copy.112
  809.5 3.3 fusion.65
  812.8 2.2 copy.112
  820.9 3.3 fusion.65
  832.2 3.3 fusion.65
  835.5 2.2 copy.112
  843.6 3.3 fusion.65
  846.9 2.2 copy.112
  854.9 3.3 fusion.65
  858.2 2.2 copy.112
  866.3 3.3 fusion.65
  869.6 2.2 copy.112
  876.0 11.6 rev.6
  887.6 219.1 %all-gather.7.cloned.1.call-done = f32[128,8,4096]{2,1,0:T(8,128)} async-done(((f32[1,8,4096]{2,1,0:T(8,128)}), f32[128,8,4096]{2,1,0:T(8,128)}) %all-gather.7.cloned.1.call-update) | async-done | bytes 16777232 | tf_op jit(solution)/shard_map/all_gather | solution.py:16
  1106.7 11.6 rev.7
  1118.3 138.6 %while.85 = (s32[]{:T(128)}, f32[8,4096]{1,0:T(8,128)S(1)}, s32[]{:T(128)}, f32[128,8,4096]{2,1,0:T(8,128)}, f32[128,8,4096]{2,1,0:T(8,128)}, /*index=5*/s32[]{:T(128)}, s32[]{:T(128)}) while((s32[]{:T(128)}, f32[8,4096]{1,0:T(8,128)S(1)}, s32[]{:T(128)}, f32[128,8,4096]{2,1,0:T(8,128)}, f32[128,8,4096]{2,1,0:T(8,128)}, ...), condition=%wide.region_17.18_spmd.clone, body=%wide.region_16.17_spmd.clone.sunk | while | flops 131076 | bytes 524389 | solution.py:28
  1258.5 15.1 while.81
  1279.1 765.4 %all-reduce.3.cloned.1.call-done = f32[8,4096]{1,0:T(8,128)} async-done(((f32[8,4096]{1,0:T(8,128)}), f32[8,4096]{1,0:T(8,128)}) %all-reduce.3.cloned.1.call-update) | async-done | bytes 131088 | tf_op jit(solution)/shard_map/psum | solution.py:141
  (500 shorter events, 418.9 us)
Async XLA Ops:
  7.2 370.8 %all-gather.5.cloned.1.call-start = ((), (), s32[]{:S(2)}) async-start(), calls=%async_computation | async-start | bytes 16908288 | tf_op jit(solution)/shard_map/all_gather | solution.py:16
  142.0 2.9 copy-start.4
  144.8 465.0 %all-gather.9.cloned.1.call-start = ((), (), s32[]{:S(2)}) async-start(), calls=%async_computation.3 | async-start | bytes 16908288 | tf_op jit(solution)/shard_map/all_gather | solution.py:16
  145.6 961.1 %all-gather.7.cloned.1.call-start = ((), (), s32[]{:S(2)}) async-start(), calls=%async_computation.1 | async-start | bytes 16908288 | tf_op jit(solution)/shard_map/all_gather | solution.py:16
  749.9 13.5 copy-start.1
  766.5 1.9 copy-start.6
  875.9 11.6 copy-start.5
  876.0 1168.6 %all-reduce.3.cloned.1.call-start = ((), (), s32[]{:S(2)}) async-start(), calls=%async_computation.2 | async-start | bytes 262144 | tf_op jit(solution)/shard_map/psum | solution.py:141
  1256.9 16.8 copy-start
  1275.7 1.2 copy-start.2
  1275.7 1.5 copy-start.3
Sparse Core Ops, SparseCore 0:
  145.0 232.9 all-gather.4
  380.4 229.4 all-gather.8
  876.1 230.5 all-gather.6
  1109.8 934.7 all-reduce.2
where the time goes:
time: 2060 us; the launch traced here: 2050 us
  waiting for transfers between devices  1450 us (70%)
  other arithmetic  347 us (17%)
  local copies, waits for them, and re-layouts  175 us (8%)
  matrix products  56.1 us (3%)
    psum x1, waiting for transfers between devices, on_device(): grad_residue = lax.psum(join_blocks(residue_term), 'ctx')  765 us
    all_gather x3, waiting for transfers between devices, carried_in(): pieces = jax.tree.map(lambda part: lax.all_gather(part, axis), value)  683 us
    select_n x254, other arithmetic, turn(): jnp.where(position < mine, new, old)  272 us
    dynamic_update_slice x48, local copies, waits for them, and re-layouts, on_device(): lax.map(forward_local, (product_blocks, decay_blocks, residue_blocks))  75.2 us
  transfers between devices with their start and end apart: 4, of which 4 were waited for; matrix products, arithmetic and copies ran while one was open for 9% of the time, Pallas kernels for 0%

commit v1 on v0

v1 whole, which is shorter than its diff:
```python
import functools

import jax
import jax.numpy as jnp
from jax import lax
from jax.experimental import pallas as pl
from jax.experimental.pallas import tpu as pltpu
from jax.sharding import Mesh, PartitionSpec as P

D = 8192
MODES = 8
norm_eps = 1e-05

LANES = 128
SUB = 8
ROWS16 = 16

CHIP_AXES = ("x", "yl", "z")
CTX_AXES = CHIP_AXES + ("core",)
CTX_SIZES = (4, 2, 8, 2)

f32 = jnp.float32
bf16 = jnp.bfloat16


def call(body, out_shape, *args, scratch=()):
    vmem = pl.BlockSpec(memory_space=pltpu.VMEM)
    return pl.pallas_call(
        body,
        out_shape=out_shape,
        in_specs=[vmem] * len(args),
        out_specs=jax.tree.map(lambda _: vmem, out_shape),
        scratch_shapes=list(scratch),
        compiler_params=pltpu.CompilerParams(vmem_limit_bytes=48 * 1024 * 1024),
    )(*args)


def shaped(*extent, dtype=f32):
    return jax.ShapeDtypeStruct(extent, dtype)


def dense_rows(group, first, tokens):
    return pl.ds(((group // SUB) * tokens + first) * SUB + group % SUB, SUB, stride=SUB)


def each_tile(tokens, groups, body, start=None, finish=None):
    def rows(tile, nothing):
        first = pl.multiple_of(tile * ROWS16, ROWS16)
        carried = start() if start else None
        for group in range(groups):
            carried = body(first, group, carried)
        if finish:
            finish(first, carried)
        return nothing

    lax.fori_loop(0, tokens // ROWS16, rows, 0)


def load_dense(ref, group, first, tokens):
    return jnp.concatenate(
        [ref[dense_rows(group, first + shift, tokens), :] for shift in (0, SUB)], axis=0
    )


def store_dense(ref, group, first, tokens, value):
    for shift in (0, SUB):
        ref[dense_rows(group, first + shift, tokens), :] = value[shift : shift + SUB]


def lanes_of(group):
    return pl.ds(group * LANES, LANES)


def tile_of(ref, first, group):
    return ref[pl.ds(first, ROWS16), lanes_of(group)].astype(f32)


def modes_of(ref, block, groups):
    return [ref[pl.ds(mode * groups + block * SUB, SUB), :] for mode in range(MODES)]


def put_modes(ref, block, groups, values):
    for mode in range(MODES):
        ref[pl.ds(mode * groups + block * SUB, SUB), :] = values[mode]


def tree_sum(terms):
    while len(terms) > 1:
        terms = [a + b for a, b in zip(terms[::2], terms[1::2])]
    return terms[0]


UNROLL = 8


def over_tokens(tokens, step, carried, backward=False):
    def several(turn, carried):
        for inner in range(UNROLL):
            at = turn * UNROLL + inner
            carried = step(tokens - 1 - at if backward else at, carried)
        return carried

    return lax.fori_loop(0, tokens // UNROLL, several, carried)


def token_row(block, token, tokens):
    return pl.ds(pl.multiple_of((block * tokens + token) * SUB, SUB), SUB)


def local_ends(tokens, groups, key, value, decay, scale, residue, product, keep, send, shrink, weight, scale_dense, whole, ends):
    for group in range(groups):
        rows = pl.ds(group, MODES, stride=groups)
        rate = decay[:, lanes_of(group)]
        in_scale = scale[:, lanes_of(group)]
        shrink[rows, :] = jnp.exp(-rate)
        whole[rows, :] = jnp.exp(-rate * tokens)
        scale_dense[rows, :] = in_scale
        weight[rows, :] = in_scale * residue[:, lanes_of(group)]

    def multiply(first, group, carried):
        store_dense(product, group, first, tokens, tile_of(key, first, group) * tile_of(value, first, group))

    each_tile(tokens, groups, multiply)
    blocks = groups // SUB
    for block in range(blocks):
        ratio = modes_of(shrink, block, groups)

        def step(token, states):
            row = product[token_row(block, token, tokens), :]
            return [r * s + row for r, s in zip(ratio, states)]

        zeros = [jnp.zeros((SUB, LANES), f32)] * MODES
        put_modes(ends, block, groups, over_tokens(tokens, step, zeros))
    core = lax.axis_index("core")
    half = MODES * groups // 2
    keep[...] = ends[pl.ds(pl.multiple_of(core * half, half), half), :]
    send[...] = ends[pl.ds(pl.multiple_of((1 - core) * half, half), half), :]


def my_half(ref, half):
    return ref[pl.ds(pl.multiple_of(lax.axis_index("core") * half, half), half), :]


def chip_total(backward, half, whole, keep, recv, total):
    core = lax.axis_index("core")
    mine_is_farther = core == (1 if backward else 0)
    mine, other = keep[...], recv[...]
    farther = jnp.where(mine_is_farther, mine, other)
    nearer = jnp.where(mine_is_farther, other, mine)
    total[...] = my_half(whole, half) * farther + nearer


def chip_scan(backward, chips, whole_cut, totals, before):
    position = lax.axis_index(CHIP_AXES)
    core = lax.axis_index("core")
    ratio = whole_cut[core * chips + position]
    ratio = ratio * ratio

    def step(turn, state):
        at = chips - 1 - turn if backward else turn
        before[at] = state
        return ratio * state + totals[at]

    lax.fori_loop(0, chips, step, jnp.zeros_like(ratio), unroll=8)


def chip_scan_and_sum(chips, whole_cut, totals, before):
    position = lax.axis_index(CHIP_AXES)
    core = lax.axis_index("core")
    ratio = whole_cut[core * chips + position]
    ratio = ratio * ratio

    def step(turn, carried):
        state, total = carried
        at = chips - 1 - turn
        before[at, 0] = state
        return ratio * state + totals[at, 0], total + totals[at, 1]

    zero = jnp.zeros_like(ratio)
    _, total = lax.fori_loop(0, chips, step, (zero, zero), unroll=8)
    before[:, 1] = jnp.broadcast_to(total[None], before[:, 1].shape)


def core_states(backward, half, whole, chip_state, keep, recv, mine, other):
    core = lax.axis_index("core")
    mine_is_farther = core == (1 if backward else 0)
    farther = jnp.where(mine_is_farther, keep[...], recv[...])
    first = chip_state[...]
    second = my_half(whole, half) * first + farther
    mine[...] = jnp.where(mine_is_farther, first, second)
    other[...] = jnp.where(mine_is_farther, second, first)


def join_halves(ref, half, mine, other):
    core = lax.axis_index("core")
    ref[pl.ds(pl.multiple_of(core * half, half), half), :] = mine
    ref[pl.ds(pl.multiple_of((1 - core) * half, half), half), :] = other


def filter_rows(tokens, groups, product, shrink, weight, entry_mine, entry_other, query, grad, gain, filtered, sums, entry, squares, dots):
    join_halves(entry, MODES * groups // 2, entry_mine[...], entry_other[...])
    for block in range(groups // SUB):
        ratio = modes_of(shrink, block, groups)
        factor = modes_of(weight, block, groups)

        def step(token, states):
            at = token_row(block, token, tokens)
            row = product[at, :]
            states = [r * s + row for r, s in zip(ratio, states)]
            filtered[at, :] = tree_sum([w * s for w, s in zip(factor, states)])
            return states

        over_tokens(tokens, step, modes_of(entry, block, groups))

    def add(first, group, carried):
        gated = tile_of(query, first, group) * load_dense(filtered, group, first, tokens)
        weighted = gain[:, lanes_of(group)] * tile_of(grad, first, group)
        return carried[0] + gated * gated, carried[1] + weighted * gated

    def zeros():
        zero = jnp.zeros((ROWS16, LANES), f32)
        return zero, zero

    def keep(first, carried):
        squares[pl.ds(first, ROWS16), :] = carried[0]
        dots[pl.ds(first, ROWS16), :] = carried[1]

    each_tile(tokens, groups, add, zeros, keep)
    sums[0:1, :] = jnp.sum(squares[...].T, axis=0, keepdims=True)
    sums[1:2, :] = jnp.sum(dots[...].T, axis=0, keepdims=True)


def norm_and_adjoint(tokens, groups, sums, other_sums, filtered, product, shrink, weight, scale_dense, entry_mine, entry_other, query, grad, gain,
                     normed, grad_query, grad_product, keep, send, entry, inverse, slope, grad_filtered, leading, residue_term):
    join_halves(entry, MODES * groups // 2, entry_mine[...], entry_other[...])
    both = sums[...] + other_sums[...]
    rms = jnp.sqrt(both[0:1] / D + norm_eps)
    inverse[...] = jnp.broadcast_to(1.0 / rms, (LANES, tokens)).T
    slope[...] = jnp.broadcast_to(both[1:2] / (D * rms * rms * rms), (LANES, tokens)).T

    def finish(first, group, carried):
        rows = pl.ds(first, ROWS16)
        part = load_dense(filtered, group, first, tokens)
        asked = tile_of(query, first, group)
        gated = asked * part
        gains = gain[:, lanes_of(group)]
        scale = inverse[rows, :]
        normed[rows, lanes_of(group)] = (gated * gains * scale).astype(bf16)
        grad_gated = gains * tile_of(grad, first, group) * scale - gated * slope[rows, :]
        grad_query[rows, lanes_of(group)] = (grad_gated * part).astype(bf16)
        store_dense(grad_filtered, group, first, tokens, grad_gated * asked)

    each_tile(tokens, groups, finish)
    for block in range(groups // SUB):
        ratio = modes_of(shrink, block, groups)
        factor = modes_of(weight, block, groups)

        def step(token, carried):
            states, terms = carried
            at = token_row(block, token, tokens)
            row = grad_filtered[at, :]
            put_in = product[at, :]
            states = [r * s + row for r, s in zip(ratio, states)]
            terms = [q + put_in * s for q, s in zip(terms, states)]
            grad_product[at, :] = tree_sum([w * s for w, s in zip(factor, states)])
            return states, terms

        zeros = [jnp.zeros((SUB, LANES), f32)] * MODES
        states, terms = over_tokens(tokens, step, (zeros, zeros), backward=True)
        put_modes(leading, block, groups, states)
        put_modes(
            residue_term,
            block,
            groups,
            [
                i * (q + r * s * e)
                for i, q, r, s, e in zip(
                    modes_of(scale_dense, block, groups), terms, ratio, states, modes_of(entry, block, groups)
                )
            ],
        )
    half = MODES * groups // 2
    core = lax.axis_index("core")
    mine = pl.ds(pl.multiple_of(core * half, half), half)
    other = pl.ds(pl.multiple_of((1 - core) * half, half), half)
    keep[0], keep[1] = leading[mine, :], residue_term[mine, :]
    send[0], send[1] = leading[other, :], residue_term[other, :]


def chip_total_and_sum(half, chips, whole, keep, recv, total):
    core = lax.axis_index("core")
    mine, other = keep[0], recv[0]
    farther = jnp.where(core == 1, mine, other)
    nearer = jnp.where(core == 1, other, mine)
    cut = half // chips
    total[:, 0] = (my_half(whole, half) * farther + nearer).reshape(chips, cut, LANES)
    total[:, 1] = (keep[1] + recv[1]).reshape(chips, cut, LANES)


def core_states_and_sum(half, chips, whole, chip_state, keep, recv, mine, other):
    core = lax.axis_index("core")
    farther = jnp.where(core == 1, keep[0], recv[0])
    first = chip_state[:, 0].reshape(half, LANES)
    second = my_half(whole, half) * first + farther
    mine[0] = jnp.where(core == 1, first, second)
    other[0] = jnp.where(core == 1, second, first)
    summed = chip_state[:, 1].reshape(half, LANES)
    mine[1] = summed
    other[1] = summed


def grad_rows(tokens, groups, grad_product, shrink, weight, after_mine, after_other, key, value, grad_key, grad_value, grad_residue, after, total, dense):
    half = MODES * groups // 2
    join_halves(after, half, after_mine[0], after_other[0])
    join_halves(total, half, after_mine[1], after_other[1])
    for group in range(groups):
        grad_residue[:, lanes_of(group)] = total[pl.ds(group, MODES, stride=groups), :]
    for block in range(groups // SUB):
        ratio = modes_of(shrink, block, groups)

        def step(token, states):
            at = token_row(block, token, tokens)
            states = [r * s for r, s in zip(ratio, states)]
            dense[at, :] = tree_sum(states) + grad_product[at, :]
            return states

        start = [w * a for w, a in zip(modes_of(weight, block, groups), modes_of(after, block, groups))]
        over_tokens(tokens, step, start, backward=True)

    def finish(first, group, carried):
        rows = pl.ds(first, ROWS16)
        part = load_dense(dense, group, first, tokens)
        grad_key[rows, lanes_of(group)] = (part * tile_of(value, first, group)).astype(bf16)
        grad_value[rows, lanes_of(group)] = (part * tile_of(key, first, group)).astype(bf16)

    each_tile(tokens, groups, finish)


def swap(value, axis):
    return lax.ppermute(value, axis, [(0, 1), (1, 0)])


def on_device(query_rows, key_rows, value_rows, decay_rate, residue, norm_gain, grad_out):
    tokens, channels = query_rows.shape
    groups = channels // LANES
    rows = MODES * groups
    half = rows // 2
    chips = lax.axis_size(CHIP_AXES)
    cut = half // chips
    gain = norm_gain[None, :]
    in_scale = jnp.sqrt(-jnp.expm1(-2.0 * decay_rate))
    dense = shaped(tokens * groups, LANES)
    modal = shaped(rows, LANES)
    halved = shaped(half, LANES)
    two_halves = shaped(2, half, LANES)
    modal_scratch = pltpu.VMEM((rows, LANES), f32)
    square_scratch = pltpu.VMEM((tokens, LANES), f32)
    dense_scratch = pltpu.VMEM((tokens * groups, LANES), f32)
    bind = functools.partial

    product, keep, send, shrink, weight, scale_dense, whole = call(
        bind(local_ends, tokens, groups),
        (dense, halved, halved, modal, modal, modal, modal),
        key_rows, value_rows, decay_rate, in_scale, residue,
        scratch=[modal_scratch],
    )
    whole_cut = whole.reshape(2 * chips, cut, LANES)
    recv = swap(send, "core")
    total = call(bind(chip_total, False, half), halved, whole, keep, recv)
    totals = lax.all_to_all(total.reshape(chips, cut, LANES), CHIP_AXES, 0, 0)
    before = call(bind(chip_scan, False, chips), shaped(chips, cut, LANES), whole_cut, totals)
    chip_state = lax.all_to_all(before, CHIP_AXES, 0, 0).reshape(half, LANES)
    entry_mine, entry_send = call(bind(core_states, False, half), (halved, halved), whole, chip_state, keep, recv)
    entry_other = swap(entry_send, "core")

    filtered, sums = call(
        bind(filter_rows, tokens, groups),
        (dense, shaped(2, tokens)),
        product, shrink, weight, entry_mine, entry_other, query_rows, grad_out, gain,
        scratch=[modal_scratch, square_scratch, square_scratch],
    )
    other_sums = swap(sums, "tp")

    normed_out, grad_query, grad_product, keep, send = call(
        bind(norm_and_adjoint, tokens, groups),
        (shaped(tokens, channels, dtype=bf16), shaped(tokens, channels, dtype=bf16), dense, two_halves, two_halves),
        sums, other_sums, filtered, product, shrink, weight, scale_dense, entry_mine, entry_other, query_rows, grad_out, gain,
        scratch=[modal_scratch, square_scratch, square_scratch, dense_scratch, modal_scratch, modal_scratch],
    )
    recv = swap(send, "core")
    total = call(bind(chip_total_and_sum, half, chips), shaped(chips, 2, cut, LANES), whole, keep, recv)
    totals = lax.all_to_all(total, CHIP_AXES, 0, 0)
    before = call(bind(chip_scan_and_sum, chips), shaped(chips, 2, cut, LANES), whole_cut, totals)
    chip_state = lax.all_to_all(before, CHIP_AXES, 0, 0)
    after_mine, after_send = call(
        bind(core_states_and_sum, half, chips), (two_halves, two_halves), whole, chip_state, keep, recv
    )
    after_other = swap(after_send, "core")

    grad_key, grad_value, grad_residue = call(
        bind(grad_rows, tokens, groups),
        (shaped(tokens, channels, dtype=bf16), shaped(tokens, channels, dtype=bf16), shaped(MODES, channels)),
        grad_product, shrink, weight, after_mine, after_other, key_rows, value_rows,
        scratch=[modal_scratch, modal_scratch, dense_scratch],
    )
    return (normed_out, grad_query, grad_key, grad_value, grad_residue)


def solution(mesh):
    devices = mesh.devices
    cut_mesh = Mesh(devices.reshape(CTX_SIZES + (devices.shape[1],)), CTX_AXES + ("tp",))
    token_split = P(CTX_AXES, "tp")
    return jax.shard_map(
        on_device,
        mesh=cut_mesh,
        in_specs=(token_split, token_split, token_split, P(None, "tp"), P(None, "tp"), P("tp"), token_split),
        out_specs=(token_split, token_split, token_split, token_split, P(None, "tp")),
        check_vma=False,
    )
```

time: 2060 us -> 108 us (0.05)
  waiting for transfers between devices: 1450 us -> 5.08 us
  other arithmetic: 347 us -> 1.13 us
  local copies, waits for them, and re-layouts: 175 us -> 6.91 us
  blocking collectives: 5.47 us -> 62 us
  matrix products: 56.1 us -> 0 us
    psum x1 -> x0, waiting for transfers between devices: 765 us -> none  [on_device(): grad_residue = lax.psum(join_blocks(residue_term), 'ctx')]
    all_gather x3 -> x0, waiting for transfers between devices: 683 us -> none  [carried_in(): pieces = jax.tree.map(lambda part: lax.all_gather(part, axis), value)]
    select_n x254 -> x0, other arithmetic: 272 us -> none  [turn(): jnp.where(position < mine, new, old)]
    dynamic_update_slice x48 -> x0, local copies, waits for them, and re-layouts: 75.2 us -> none  [on_device(): lax.map(forward_local, (product_blocks, decay_blocks, residue_blocks))]
    all_to_all x0 -> x4, blocking collectives: none -> 62 us  [the longest x1 20.2 us: on_device(): totals = lax.all_to_all(total.reshape(chips, cut, LANES), CHIP_AXES, 0, 0)]
    dot_general x16 -> x0, matrix products: 56.1 us -> none  [the longest x8 29.7 us: forward_local(): jnp.dot(lower_ones, weighted.reshape(row_count, -1), precision=exact_mode)]
    reduce_sum x33 -> x0, other arithmetic: 45.2 us -> none  [the longest x8 16.2 us: backward_local(): jnp.sum((in_scale * residue_part)[None] * adjoint_local, axis=1)]
    rev x2 -> x0, local copies, waits for them, and re-layouts: 23.1 us -> none  [carried_in(): pieces = jax.tree.map(lambda part: part[::-1], pieces)]
  transfers between devices with their start and end apart: 4 -> 5, of which waited for: 4 -> 5; matrix products, arithmetic and copies ran while one was open for 9% -> 0% of each run, Pallas kernels for 0% -> 0%
where the time goes in v1:
time: 108 us
  blocking collectives  62 us (57%)
  Pallas kernels  19 us (18%)
  starting transfers between devices  13 us (12%)
  local copies, waits for them, and re-layouts  6.91 us (6%)
  waiting for transfers between devices  5.08 us (5%)
  other arithmetic  1.13 us (1%)
    all_to_all x1, blocking collectives, on_device(): totals = lax.all_to_all(total.reshape(chips, cut, LANES), CHIP_AXES, 0, 0)  20.2 us
    pallas_call x10, Pallas kernels, call(): pl.pallas_call(body, out_shape=out_shape, in_specs=[vmem] * len(args), ou...  19 us
    all_to_all x1, blocking collectives, on_device(): chip_state = lax.all_to_all(before, CHIP_AXES, 0, 0)  14.4 us
    all_to_all x1, blocking collectives, on_device(): totals = lax.all_to_all(total, CHIP_AXES, 0, 0)  14.2 us
    all_to_all x1, blocking collectives, on_device(): chip_state = lax.all_to_all(before, CHIP_AXES, 0, 0).reshape(half, LANES)  13.3 us
    ppermute x5, starting transfers between devices, swap(): return lax.ppermute(value, axis, [(0, 1), (1, 0)])  13 us
    unnamed x20, local copies, waits for them, and re-layouts  6.91 us
    ppermute x5, waiting for transfers between devices, swap(): return lax.ppermute(value, axis, [(0, 1), (1, 0)])  5.08 us
  transfers between devices with their start and end apart: 5, of which 5 were waited for; matrix products, arithmetic and copies ran while one was open for 0% of the time, Pallas kernels for 0%

profile of v1, /device:TPU:1, one launch (start us, length us, event | category | flops | bytes accessed | tf_op | source)
XLA Modules:
  0.0 107.9 jit_solution(724031291249700060)
XLA Ops:
  0.6 0.0 copy-start.2
  0.6 0.0 copy-start.1
  0.7 1.1 %negate_sqrt_fusion.scale = f32[8,4096]{1,0:T(8,128)S(1)} fusion(f32[8,4096]{1,0:T(8,128)} %decay.1), kind=kLoop, calls=%fused_computation | loop fusion | flops 65536 | bytes 262144 | tf_op jit(solution)/shard_map/sqrt | solution.py:351
  1.8 0.0 copy-start.3
  1.8 1.2 %copy-done.3 = bf16[128,4096]{1,0:T(8,128)(2,1)S(1)} copy-done((bf16[128,4096]{1,0:T(8,128)(2,1)S(1)}, bf16[128,4096]{1,0:T(8,128)(2,1)}, u32[]{:S(2)}) %copy-start.3) | copy-done | bytes 1048600
  3.0 0.0 copy-start.5
  3.0 1.2 %copy-done.5 = bf16[128,4096]{1,0:T(8,128)(2,1)S(1)} copy-done((bf16[128,4096]{1,0:T(8,128)(2,1)S(1)}, bf16[128,4096]{1,0:T(8,128)(2,1)}, u32[]{:S(2)}) %copy-start.5) | copy-done | bytes 1048600
  4.2 0.0 copy-start.7
  4.2 0.9 copy-done.7
  5.1 0.0 copy-start.8
  5.1 0.9 copy-done.8
  6.0 0.0 copy-start.9
  6.1 2.0 %shard_map.110 = (f32[4096,128]{1,0:T(8,128)S(1)}, f32[128,128]{1,0:T(8,128)S(1)}, f32[128,128]{1,0:T(8,128)S(1)}, f32[256,128]{1,0:T(8,128)S(1)}, f32[256,128]{...) custom-call(bf16[128,4096]{1,0:T(8,128)(2,1)S(1)} %copy-done.3, bf16[128,4096]{1,0:T(8,128)(2,1)S(1)} %copy-done.5, ...), custom_call_target="tpu_custom_call" | custom-call | tf_op jit(solution)/shard_map/pallas_call | solution.py:28
  8.0 0.0 copy-start
  8.0 1.3 %copy-done = f32[4096,128]{1,0:T(8,128)} copy-done((f32[4096,128]{1,0:T(8,128)}, f32[4096,128]{1,0:T(8,128)S(1)}, u32[]{:S(2)}) %copy-start) | copy-done | bytes 2097176
  9.4 3.2 %collective-permute-start = (f32[128,128]{1,0:T(8,128)S(1)}, f32[128,128]{1,0:T(8,128)S(1)}, u32[]{:S(2)}, u32[]{:S(2)}) collective-permute-start(f32[128,128]{1,0:T(8,128)S(1)} %get-tuple-element.31), channel_id=1, source_target_pairs={{0,2},{2,0},{1,3},{3,1},{4,6},{6,4},{5,7},{7,5},{8,10},{10,8},{9,1... | collective-permute-start | bytes 196616 | tf_op jit(solution)/shard_map/ppermute | solution.py:340
  12.6 0.9 collective-permute-done.recv
  13.5 20.2 %all_to_all.20.totals = f32[64,2,128]{2,1,0:T(2,128)S(1)} all-to-all(f32[64,2,128]{2,1,0:T(2,128)S(1)} %bitcast.7), channel_id=1, replica_groups=mesh['x'=4,'yl'=2,'z'=8,'core'=2,'tp'=2] {'x','yl','z'}, dimensions={0} | all-to-all | bytes 131072 | tf_op jit(solution)/shard_map/all_to_all | solution.py:370
  33.8 0.1 shard_map.112
  33.9 13.3 %all_to_all.21 = f32[64,2,128]{2,1,0:T(2,128)S(1)} all-to-all(f32[64,2,128]{2,1,0:T(2,128)S(1)} %shard_map.112), channel_id=1, replica_groups=mesh['x'=4,'yl'=2,'z'=8,'core'=2,'tp'=2] {'x','yl','z'}, dimensions={0} | all-to-all | bytes 131072 | tf_op jit(solution)/shard_map/all_to_all | solution.py:372
  47.2 3.0 %collective-permute-start.1 = (f32[128,128]{1,0:T(8,128)S(1)}, f32[128,128]{1,0:T(8,128)S(1)}, u32[]{:S(2)}, u32[]{:S(2)}) collective-permute-start(f32[128,128]{1,0:T(8,128)S(1)} %get-tuple-element.33), channel_id=1, source_target_pairs={{0,2},{2,0},{1,3},{3,1},{4,6},{6,4},{5,7},{7,5},{8,10},{10,8},{9,1... | collective-permute-start | bytes 196616 | tf_op jit(solution)/shard_map/ppermute | solution.py:340
  50.2 0.9 collective-permute-done.1.entry_other
  51.1 0.0 copy-done.2
  51.1 0.0 copy-done.1
  51.1 0.0 copy-done.9
  51.2 4.9 %shard_map.114 = (f32[4096,128]{1,0:T(8,128)S(1)}, f32[2,128]{1,0:T(2,128)S(1)}) custom-call(f32[4096,128]{1,0:T(8,128)} %copy-done, f32[256,128]{1,0:T(8,128)S(1)} %get-tuple-element.27.shrink, f32[256,128]{1,0:T(8,128)S(1)} %get-tuple-element.28.weight, f32[128,128]{1,0:T(8,128)S(1)} %get-tuple-element.32.entry_mine, ...), custom_call_target="tpu_custom_call" | custom-call | tf_op jit(solution)/shard_map/pallas_call | solution.py:28
  56.1 0.0 copy-start.6
  56.1 1.3 %copy-done.6 = f32[4096,128]{1,0:T(8,128)} copy-done((f32[4096,128]{1,0:T(8,128)}, f32[4096,128]{1,0:T(8,128)S(1)}, u32[]{:S(2)}) %copy-start.6) | copy-done | bytes 2097176
  57.4 2.6 %collective-permute-start.2 = (f32[2,128]{1,0:T(2,128)S(1)}, f32[2,128]{1,0:T(2,128)S(1)}, u32[]{:S(2)}, u32[]{:S(2)}) collective-permute-start(f32[2,128]{1,0:T(2,128)S(1)} %get-tuple-element.34.sums), channel_id=1, source_target_pairs={{0,1},{1,0},{2,3},{3,2},{4,5},{5,4},{6,7},{7,6},{8,9},{9,8},{10,11... | collective-permute-start | bytes 3080 | tf_op jit(solution)/shard_map/ppermute | solution.py:340
  60.0 1.3 %collective-permute-done.2.other_sums = f32[2,128]{1,0:T(2,128)S(1)} collective-permute-done((f32[2,128]{1,0:T(2,128)S(1)}, f32[2,128]{1,0:T(2,128)S(1)}, u32[]{:S(2)}, u32[]{:S(2)}) %collective-permute-start.2) | collective-permute-done | bytes 1056 | tf_op jit(solution)/shard_map/ppermute | solution.py:340
  61.3 8.3 %shard_map.115 = (bf16[128,4096]{1,0:T(8,128)(2,1)}, bf16[128,4096]{1,0:T(8,128)(2,1)}, f32[4096,128]{1,0:T(8,128)S(1)}, f32[2,128,128]{2,1,0:T(8,128)S(1)}, f32[2,128,128]{2,1,0:T(8,128)S(1)}) custom-call(f32[2,128]{1,0:T(2,128)S(1)} %get-tuple-element.34.sums, f32[2,128]{1,0:T(2,128)S(1)} %collective-permute-done.2.other_sums, f32[4096,128]{1,0:T(8,128)} %copy-done.6, ...), custom_call_target="tpu_custom_call" | custom-call | tf_op jit(solution)/shard_map/pallas_call | solution.py:28
  69.6 0.0 copy-start.4
  69.6 1.5 %collective-permute-start.3 = (f32[2,128,128]{2,1,0:T(8,128)S(1)}, f32[2,128,128]{2,1,0:T(8,128)S(1)}, u32[]{:S(2)}, u32[]{:S(2)}) collective-permute-start(f32[2,128,128]{2,1,0:T(8,128)S(1)} %get-tuple-element.41), channel_id=1, source_target_pairs={{0,2},{2,0},{1,3},{3,1},{4,6},{6,4},{5,7},{7,5},{8,10},{10,8},{9,1... | collective-permute-start | bytes 393224 | tf_op jit(solution)/shard_map/ppermute | solution.py:340
  71.1 1.0 collective-permute-done.3.recv
  72.2 14.2 %all_to_all.22.totals = f32[64,2,2,128]{3,2,1,0:T(2,128)S(1)} all-to-all(f32[64,2,2,128]{3,2,1,0:T(2,128)S(1)} %shard_map.116), channel_id=1, replica_groups=mesh['x'=4,'yl'=2,'z'=8,'core'=2,'tp'=2] {'x','yl','z'}, dimensions={0} | all-to-all | bytes 262144 | tf_op jit(solution)/shard_map/all_to_all | solution.py:392
  86.3 0.2 shard_map.117
  86.5 14.4 %all_to_all.23.chip_state = f32[64,2,2,128]{3,2,1,0:T(2,128)S(1)} all-to-all(f32[64,2,2,128]{3,2,1,0:T(2,128)S(1)} %shard_map.117), channel_id=1, replica_groups=mesh['x'=4,'yl'=2,'z'=8,'core'=2,'tp'=2] {'x','yl','z'}, dimensions={0} | all-to-all | bytes 262144 | tf_op jit(solution)/shard_map/all_to_all | solution.py:394
  100.8 0.1 shard_map.118
  100.9 2.6 %collective-permute-start.4 = (f32[2,128,128]{2,1,0:T(8,128)S(1)}, f32[2,128,128]{2,1,0:T(8,128)S(1)}, u32[]{:S(2)}, u32[]{:S(2)}) collective-permute-start(f32[2,128,128]{2,1,0:T(8,128)S(1)} %get-tuple-element.43), channel_id=1, source_target_pairs={{0,2},{2,0},{1,3},{3,1},{4,6},{6,4},{5,7},{7,5},{8,10},{10,8},{9,1... | collective-permute-start | bytes 393224 | tf_op jit(solution)/shard_map/ppermute | solution.py:340
  103.5 1.0 collective-permute-done.4.after_other
  104.5 0.0 copy-done.4
  104.5 3.4 %shard_map.119 = (bf16[128,4096]{1,0:T(8,128)(2,1)}, bf16[128,4096]{1,0:T(8,128)(2,1)}, f32[8,4096]{1,0:T(8,128)}) custom-call(f32[4096,128]{1,0:T(8,128)S(1)} %get-tuple-element.39.grad_product, f32[256,128]{1,0:T(8,128)S(1)} %get-tuple-element.27.shrink, f32[256,128]{1,0:T(8,128)S(1)} %get-tuple-element.28.weight, ...), custom_call_target="tpu_custom_call" | custom-call | tf_op jit(solution)/shard_map/pallas_call | solution.py:28
  (3 shorter events, 0.1 us)
Async XLA Ops:
  0.6 50.5 %copy-start.2 = (bf16[128,4096]{1,0:T(8,128)(2,1)S(1)}, bf16[128,4096]{1,0:T(8,128)(2,1)}, u32[]{:S(2)}) copy-start(bf16[128,4096]{1,0:T(8,128)(2,1)} %grad.3) | copy-start | bytes 3145732
  0.6 50.5 %copy-start.1 = (bf16[128,4096]{1,0:T(8,128)(2,1)S(1)}, bf16[128,4096]{1,0:T(8,128)(2,1)}, u32[]{:S(2)}) copy-start(bf16[128,4096]{1,0:T(8,128)(2,1)} %query.3) | copy-start | bytes 3145732
  1.8 1.2 %copy-start.3 = (bf16[128,4096]{1,0:T(8,128)(2,1)S(1)}, bf16[128,4096]{1,0:T(8,128)(2,1)}, u32[]{:S(2)}) copy-start(bf16[128,4096]{1,0:T(8,128)(2,1)} %key.3) | copy-start | bytes 3145732
  3.0 1.2 %copy-start.5 = (bf16[128,4096]{1,0:T(8,128)(2,1)S(1)}, bf16[128,4096]{1,0:T(8,128)(2,1)}, u32[]{:S(2)}) copy-start(bf16[128,4096]{1,0:T(8,128)(2,1)} %value.3) | copy-start | bytes 3145732
  4.2 0.9 copy-start.7
  5.1 0.9 copy-start.8
  6.0 45.1 %copy-start.9 = (f32[4096]{0:T(1024)S(1)}, f32[4096]{0:T(1024)}, u32[]{:S(2)}) copy-start(f32[4096]{0:T(1024)} %param.12) | copy-start | bytes 49156
  8.0 1.3 %copy-start = (f32[4096,128]{1,0:T(8,128)}, f32[4096,128]{1,0:T(8,128)S(1)}, u32[]{:S(2)}) copy-start(f32[4096,128]{1,0:T(8,128)S(1)} %get-tuple-element.26.product) | copy-start | bytes 6291460
  9.4 4.1 %collective-permute-start = (f32[128,128]{1,0:T(8,128)S(1)}, f32[128,128]{1,0:T(8,128)S(1)}, u32[]{:S(2)}, u32[]{:S(2)}) collective-permute-start(f32[128,128]{1,0:T(8,128)S(1)} %get-tuple-element.31), channel_id=1, source_target_pairs={{0,2},{2,0},{1,3},{3,1},{4,6},{6,4},{5,7},{7,5},{8,10},{10,8},{9,1... | collective-permute-start | bytes 196616 | tf_op jit(solution)/shard_map/ppermute | solution.py:340
  47.2 3.9 %collective-permute-start.1 = (f32[128,128]{1,0:T(8,128)S(1)}, f32[128,128]{1,0:T(8,128)S(1)}, u32[]{:S(2)}, u32[]{:S(2)}) collective-permute-start(f32[128,128]{1,0:T(8,128)S(1)} %get-tuple-element.33), channel_id=1, source_target_pairs={{0,2},{2,0},{1,3},{3,1},{4,6},{6,4},{5,7},{7,5},{8,10},{10,8},{9,1... | collective-permute-start | bytes 196616 | tf_op jit(solution)/shard_map/ppermute | solution.py:340
  56.1 1.3 %copy-start.6 = (f32[4096,128]{1,0:T(8,128)}, f32[4096,128]{1,0:T(8,128)S(1)}, u32[]{:S(2)}) copy-start(f32[4096,128]{1,0:T(8,128)S(1)} %get-tuple-element.35.filtered) | copy-start | bytes 6291460
  57.4 3.9 %collective-permute-start.2 = (f32[2,128]{1,0:T(2,128)S(1)}, f32[2,128]{1,0:T(2,128)S(1)}, u32[]{:S(2)}, u32[]{:S(2)}) collective-permute-start(f32[2,128]{1,0:T(2,128)S(1)} %get-tuple-element.34.sums), channel_id=1, source_target_pairs={{0,1},{1,0},{2,3},{3,2},{4,5},{5,4},{6,7},{7,6},{8,9},{9,8},{10,11... | collective-permute-start | bytes 3080 | tf_op jit(solution)/shard_map/ppermute | solution.py:340
  69.6 34.9 %copy-start.4 = (bf16[128,4096]{1,0:T(8,128)(2,1)S(1)}, bf16[128,4096]{1,0:T(8,128)(2,1)}, u32[]{:S(2)}) copy-start(bf16[128,4096]{1,0:T(8,128)(2,1)} %key.3) | copy-start | bytes 3145732
  69.6 2.5 %collective-permute-start.3 = (f32[2,128,128]{2,1,0:T(8,128)S(1)}, f32[2,128,128]{2,1,0:T(8,128)S(1)}, u32[]{:S(2)}, u32[]{:S(2)}) collective-permute-start(f32[2,128,128]{2,1,0:T(8,128)S(1)} %get-tuple-element.41), channel_id=1, source_target_pairs={{0,2},{2,0},{1,3},{3,1},{4,6},{6,4},{5,7},{7,5},{8,10},{10,8},{9,1... | collective-permute-start | bytes 393224 | tf_op jit(solution)/shard_map/ppermute | solution.py:340
  100.9 3.6 %collective-permute-start.4 = (f32[2,128,128]{2,1,0:T(8,128)S(1)}, f32[2,128,128]{2,1,0:T(8,128)S(1)}, u32[]{:S(2)}, u32[]{:S(2)}) collective-permute-start(f32[2,128,128]{2,1,0:T(8,128)S(1)} %get-tuple-element.43), channel_id=1, source_target_pairs={{0,2},{2,0},{1,3},{3,1},{4,6},{6,4},{5,7},{7,5},{8,10},{10,8},{9,1... | collective-permute-start | bytes 393224 | tf_op jit(solution)/shard_map/ppermute | solution.py:340

commit v2 on v1

v2 whole, which is shorter than its diff:
```python
import functools

import jax
import jax.numpy as jnp
from jax import lax
from jax.experimental import pallas as pl
from jax.experimental.pallas import tpu as pltpu
from jax.sharding import Mesh, PartitionSpec as P

D = 8192
MODES = 8
HALF_MODES = MODES // 2
norm_eps = 1e-05

LANES = 128
SUB = 8
ROWS16 = 16
UNROLL = 8
CHUNKS = 4

CHIP_AXES = ("x", "yl", "z")
CTX_AXES = CHIP_AXES + ("core",)
CTX_SIZES = (4, 2, 8, 2)

f32 = jnp.float32
bf16 = jnp.bfloat16

in_vmem = pl.BlockSpec(memory_space=pltpu.VMEM)
in_hbm = pl.BlockSpec(memory_space=pltpu.HBM)


def call(body, out_shape, *args, scratch=(), in_specs=None, out_specs=None):
    return pl.pallas_call(
        body,
        out_shape=out_shape,
        in_specs=in_specs or [in_vmem] * len(args),
        out_specs=out_specs or jax.tree.map(lambda _: in_vmem, out_shape),
        scratch_shapes=list(scratch),
        compiler_params=pltpu.CompilerParams(vmem_limit_bytes=20 * 1024 * 1024),
    )(*args)


def shaped(*extent, dtype=f32):
    return jax.ShapeDtypeStruct(extent, dtype)


def dense_rows(group, first, tokens):
    return pl.ds(((group // SUB) * tokens + first) * SUB + group % SUB, SUB, stride=SUB)


def each_tile(first_tile, tiles, groups, body):
    def rows(tile, nothing):
        first = pl.multiple_of(tile * ROWS16, ROWS16)
        for group in range(groups):
            body(first, group)
        return nothing

    lax.fori_loop(first_tile, first_tile + tiles, rows, 0)


def load_dense(ref, group, first, tokens):
    return jnp.concatenate(
        [ref[dense_rows(group, first + shift, tokens), :] for shift in (0, SUB)], axis=0
    )


def store_dense(ref, group, first, tokens, value):
    for shift in (0, SUB):
        ref[dense_rows(group, first + shift, tokens), :] = value[shift : shift + SUB]


def lanes_of(group):
    return pl.ds(group * LANES, LANES)


def tile_of(ref, first, group):
    return ref[pl.ds(first, ROWS16), lanes_of(group)].astype(f32)


def half_rows(block, mode, groups):
    return pl.ds(mode * groups + block * SUB, SUB)


def half_of(ref, block, groups):
    return [ref[half_rows(block, mode, groups), :] for mode in range(HALF_MODES)]


def core_half(ref, block, groups, mine):
    core = lax.axis_index("core")
    first = (core if mine else 1 - core) * (HALF_MODES * groups)
    return [
        ref[pl.ds(pl.multiple_of(first + mode * groups + block * SUB, SUB), SUB), :]
        for mode in range(HALF_MODES)
    ]


def both_halves(ref, block, groups):
    return core_half(ref, block, groups, True) + core_half(ref, block, groups, False)


def my_rows(half):
    return pl.ds(pl.multiple_of(lax.axis_index("core") * half, half), half)


def tree_sum(terms):
    while len(terms) > 1:
        pairs = [a + b for a, b in zip(terms[::2], terms[1::2])]
        terms = pairs + terms[len(pairs) * 2 :]
    return terms[0]


def over_tokens(first, count, step, carried, backward=False):
    def several(turn, carried):
        for inner in range(UNROLL):
            at = turn * UNROLL + inner
            carried = step(first + (count - 1 - at if backward else at), carried)
        return carried

    return lax.fori_loop(0, count // UNROLL, several, carried)


def token_row(block, token, tokens):
    return pl.ds(pl.multiple_of((block * tokens + token) * SUB, SUB), SUB)


def zero_states(count):
    return [jnp.zeros((SUB, LANES), f32)] * count


def local_ends(tokens, groups, key, value, decay, residue, gain, product, keep, send, shrink, whole, weight, scale_dense, gain_in,
               key_in, value_in, rate_in, residue_in, whole_all, arrived):
    whole_copies = [
        pltpu.make_async_copy(source, target, arrived.at[2 * CHUNKS + which])
        for which, (source, target) in enumerate(((decay, rate_in), (residue, residue_in), (gain, gain_in)))
    ]
    for copy in whole_copies[:2]:
        copy.start()
    some = tokens // CHUNKS
    copies = []
    for chunk in range(CHUNKS):
        rows = pl.ds(chunk * some, some)
        pair = [
            pltpu.make_async_copy(source.at[rows, :], target.at[rows, :], arrived.at[2 * chunk + which])
            for which, (source, target) in enumerate(((key, key_in), (value, value_in)))
        ]
        for copy in pair:
            copy.start()
        copies.append(pair)
    whole_copies[2].start()
    for copy in whole_copies[:2]:
        copy.wait()
    for group in range(groups):
        rows = pl.ds(group, MODES, stride=groups)
        rate = rate_in[:, lanes_of(group)]
        in_scale = jnp.sqrt(one_minus_exp_of_minus(2.0 * rate))
        shrink[rows, :] = jnp.exp(-rate)
        whole_all[rows, :] = jnp.exp(-rate * tokens)
        scale_dense[rows, :] = in_scale
        weight[rows, :] = in_scale * residue_in[:, lanes_of(group)]
    whole[...] = whole_all[my_rows(HALF_MODES * groups), :]

    def multiply(first, group):
        store_dense(product, group, first, tokens, tile_of(key_in, first, group) * tile_of(value_in, first, group))

    for chunk in range(CHUNKS):
        for copy in copies[chunk]:
            copy.wait()
        tiles = some // ROWS16
        each_tile(chunk * tiles, tiles, groups, multiply)
        for block in range(groups // SUB):
            ratio = both_halves(shrink, block, groups)

            def step(token, states):
                row = product[token_row(block, token, tokens), :]
                return [r * s + row for r, s in zip(ratio, states)]

            states = half_of(keep, block, groups) + half_of(send, block, groups) if chunk else zero_states(MODES)
            states = over_tokens(chunk * some, some, step, states)
            for mode in range(HALF_MODES):
                keep[half_rows(block, mode, groups), :] = states[mode]
                send[half_rows(block, mode, groups), :] = states[HALF_MODES + mode]
    whole_copies[2].wait()


def one_minus_exp_of_minus(value):
    series = 1.0 - value / 9.0
    for divisor in range(8, 1, -1):
        series = 1.0 - value / divisor * series
    return jnp.where(value < 0.25, value * series, 1.0 - jnp.exp(-value))


def prepare(tokens, groups, query, grad, gain, asked, squared):
    def multiply(first, group):
        rows = tile_of(query, first, group)
        store_dense(asked, group, first, tokens, gain[:, lanes_of(group)] * tile_of(grad, first, group) * rows)
        store_dense(squared, group, first, tokens, rows * rows)

    each_tile(0, tokens // ROWS16, groups, multiply)


def chip_total(whole, keep, recv, total):
    mine_is_farther = lax.axis_index("core") == 0
    mine, other = keep[...], recv[...]
    farther = jnp.where(mine_is_farther, mine, other)
    nearer = jnp.where(mine_is_farther, other, mine)
    total[...] = whole[...] * farther + nearer


def chip_scan(chips, whole_cut, totals, before):
    ratio = whole_cut[lax.axis_index(CHIP_AXES)]
    ratio = ratio * ratio

    def step(at, state):
        before[at] = state
        return ratio * state + totals[at]

    lax.fori_loop(0, chips, step, jnp.zeros_like(ratio), unroll=8)


def core_states(whole, chip_state, keep, recv, mine, other):
    mine_is_farther = lax.axis_index("core") == 0
    farther = jnp.where(mine_is_farther, keep[...], recv[...])
    first = chip_state[...]
    second = whole[...] * first + farther
    mine[...] = jnp.where(mine_is_farther, first, second)
    other[...] = jnp.where(mine_is_farther, second, first)


def filter_mine(tokens, groups, product, shrink, weight, entry, partial):
    for pair in range(0, groups // SUB, 2):
        blocks = (pair, pair + 1)
        ratio = [core_half(shrink, block, groups, True) for block in blocks]
        factor = [core_half(weight, block, groups, True) for block in blocks]

        def step(token, states):
            result = []
            for which, block in enumerate(blocks):
                at = token_row(block, token, tokens)
                row = product[at, :]
                now = [r * s + row for r, s in zip(ratio[which], states[which])]
                partial[at, :] = tree_sum([w * s for w, s in zip(factor[which], now)])
                result.append(now)
            return result

        over_tokens(0, tokens, step, [half_of(entry, block, groups) for block in blocks])


def filter_other(tokens, groups, product, shrink, weight, entry, partial, asked, squared, filtered, curved, sums, squares, dots):
    for pair in range(0, groups // SUB, 2):
        blocks = (pair, pair + 1)
        ratio = [core_half(shrink, block, groups, False) for block in blocks]
        factor = [core_half(weight, block, groups, False) for block in blocks]

        def step(token, states):
            result, square_terms, dot_terms = [], [], []
            for which, block in enumerate(blocks):
                at = token_row(block, token, tokens)
                row = product[at, :]
                now = [r * s + row for r, s in zip(ratio[which], states[which])]
                value = partial[at, :] + tree_sum([w * s for w, s in zip(factor[which], now)])
                bent = squared[at, :] * value
                filtered[at, :] = value
                curved[at, :] = bent
                square_terms.append(bent * value)
                dot_terms.append(asked[at, :] * value)
                result.append(now)
            rows = token_row(0, token, tokens)
            if pair:
                square_terms.append(squares[rows, :])
                dot_terms.append(dots[rows, :])
            squares[rows, :] = tree_sum(square_terms)
            dots[rows, :] = tree_sum(dot_terms)
            return result

        over_tokens(0, tokens, step, [half_of(entry, block, groups) for block in blocks])
    for line, ref in enumerate((squares, dots)):
        per_token = tree_sum([ref[pl.ds(shift, tokens, stride=SUB), :] for shift in range(SUB)])
        sums[line : line + 1, :] = jnp.sum(per_token.T, axis=0, keepdims=True)


def local_adjoint(tokens, groups, sums, other_sums, asked, curved, product, shrink, scale_dense, entry_mine, entry_other,
                  inverse, slope, grad_filtered, keep, send):
    both = sums[...] + other_sums[...]
    rms = jnp.sqrt(both[0:1] / D + norm_eps)
    inverse[...] = jnp.broadcast_to(1.0 / rms, (LANES, tokens)).T
    slope[...] = jnp.broadcast_to(both[1:2] / (D * rms * rms * rms), (LANES, tokens)).T
    for block in range(groups // SUB):
        ratio = both_halves(shrink, block, groups)

        def step(token, carried):
            states, terms = carried
            at = token_row(block, token, tokens)
            now = pl.ds(token, 1)
            row = inverse[now, :] * asked[at, :] - slope[now, :] * curved[at, :]
            grad_filtered[at, :] = row
            put_in = product[at, :]
            states = [r * s + row for r, s in zip(ratio, states)]
            terms = [q + put_in * s for q, s in zip(terms, states)]
            return states, terms

        states, terms = over_tokens(0, tokens, step, (zero_states(MODES), zero_states(MODES)), backward=True)
        entry = half_of(entry_mine, block, groups) + half_of(entry_other, block, groups)
        scale = both_halves(scale_dense, block, groups)
        terms = [i * (q + r * s * e) for i, q, r, s, e in zip(scale, terms, ratio, states, entry)]
        for mode in range(HALF_MODES):
            rows = half_rows(block, mode, groups)
            keep[0, rows, :], keep[1, rows, :] = states[mode], terms[mode]
            send[0, rows, :], send[1, rows, :] = states[HALF_MODES + mode], terms[HALF_MODES + mode]


def tile_copies(tile, sent, *pairs):
    rows = pl.ds(pl.multiple_of(tile * ROWS16, ROWS16), ROWS16)
    return [
        pltpu.make_async_copy(source.at[rows, :], target.at[rows, :], sent.at[which, tile])
        for which, (source, target) in enumerate(pairs)
    ]


def norm_rows(tokens, groups, inverse, slope, filtered, query, grad, gain, normed, grad_query, normed_out, grad_out, sent):
    pairs = ((normed_out, normed), (grad_out, grad_query))
    tiles = tokens // ROWS16

    def chunk(tile, nothing):
        first = pl.multiple_of(tile * ROWS16, ROWS16)
        rows = pl.ds(first, ROWS16)
        for group in range(groups):
            part = load_dense(filtered, group, first, tokens)
            gated = tile_of(query, first, group) * part
            gains = gain[:, lanes_of(group)]
            scale = inverse[rows, :]
            normed_out[rows, lanes_of(group)] = (gated * gains * scale).astype(bf16)
            grad_gated = gains * tile_of(grad, first, group) * scale - gated * slope[rows, :]
            grad_out[rows, lanes_of(group)] = (grad_gated * part).astype(bf16)
        for copy in tile_copies(tile, sent, *pairs):
            copy.start()
        return nothing

    lax.fori_loop(0, tiles, chunk, 0)
    for tile in range(tiles):
        for copy in tile_copies(tile, sent, *pairs):
            copy.wait()


def chip_total_and_sum(half, chips, whole, keep, recv, total):
    core = lax.axis_index("core")
    mine, other = keep[0], recv[0]
    farther = jnp.where(core == 1, mine, other)
    nearer = jnp.where(core == 1, other, mine)
    cut = half // chips
    total[:, 0] = (whole[...] * farther + nearer).reshape(chips, cut, LANES)
    total[:, 1] = (keep[1] + recv[1]).reshape(chips, cut, LANES)


def chip_scan_and_sum(chips, whole_cut, totals, before):
    ratio = whole_cut[lax.axis_index(CHIP_AXES)]
    ratio = ratio * ratio

    def step(turn, carried):
        state, total = carried
        at = chips - 1 - turn
        before[at, 0] = state
        return ratio * state + totals[at, 0], total + totals[at, 1]

    zero = jnp.zeros_like(ratio)
    _, total = lax.fori_loop(0, chips, step, (zero, zero), unroll=8)
    before[:, 1] = jnp.broadcast_to(total[None], before[:, 1].shape)


def core_states_and_sum(half, whole, chip_state, keep, recv, mine, other):
    core = lax.axis_index("core")
    farther = jnp.where(core == 1, keep[0], recv[0])
    first = chip_state[:, 0].reshape(half, LANES)
    second = whole[...] * first + farther
    mine[0] = jnp.where(core == 1, first, second)
    other[0] = jnp.where(core == 1, second, first)
    summed = chip_state[:, 1].reshape(half, LANES)
    mine[1] = summed
    other[1] = summed


def grad_mine(tokens, groups, grad_filtered, shrink, weight, after, partial):
    for pair in range(0, groups // SUB, 2):
        blocks = (pair, pair + 1)
        ratio = [core_half(shrink, block, groups, True) for block in blocks]
        factor = [core_half(weight, block, groups, True) for block in blocks]

        def step(token, states):
            result = []
            for which, block in enumerate(blocks):
                at = token_row(block, token, tokens)
                row = grad_filtered[at, :]
                now = [r * s + row for r, s in zip(ratio[which], states[which])]
                partial[at, :] = tree_sum([w * s for w, s in zip(factor[which], now)])
                result.append(now)
            return result

        over_tokens(0, tokens, step, [half_of(after.at[0], block, groups) for block in blocks], backward=True)


def grad_rows(tokens, groups, grad_filtered, shrink, weight, after_mine, after_other, partial, key, value,
              grad_key, grad_value, grad_residue, total, dense, key_out, value_out, residue_out, sent, residue_sent):
    half = HALF_MODES * groups
    core = lax.axis_index("core")
    total[my_rows(half), :] = after_mine[1]
    total[pl.ds(pl.multiple_of((1 - core) * half, half), half), :] = after_other[1]
    for group in range(groups):
        residue_out[:, lanes_of(group)] = total[pl.ds(group, MODES, stride=groups), :]
    residue_copy = pltpu.make_async_copy(residue_out, grad_residue, residue_sent)
    residue_copy.start()
    blocks = groups // SUB
    tiles = tokens // ROWS16

    pairs = ((key_out, grad_key), (value_out, grad_value))

    def chunk(turn, states):
        tile = tiles - 1 - turn
        first = pl.multiple_of(tile * ROWS16, ROWS16)
        rows = pl.ds(first, ROWS16)
        states = [list(part) for part in states]
        for block in range(blocks):
            ratio = core_half(shrink, block, groups, False)
            factor = core_half(weight, block, groups, False)
            for inner in range(ROWS16 - 1, -1, -1):
                at = token_row(block, first + inner, tokens)
                row = grad_filtered[at, :]
                states[block] = [r * s + row for r, s in zip(ratio, states[block])]
                part = partial[at, :] + tree_sum([w * s for w, s in zip(factor, states[block])])
                dense[block, inner * SUB : (inner + 1) * SUB, :] = part
            for group in range(block * SUB, (block + 1) * SUB):
                part = dense[block, pl.ds(group % SUB, ROWS16, stride=SUB), :]
                key_out[rows, lanes_of(group)] = (part * tile_of(value, first, group)).astype(bf16)
                value_out[rows, lanes_of(group)] = (part * tile_of(key, first, group)).astype(bf16)
        for copy in tile_copies(tile, sent, *pairs):
            copy.start()
        return states

    lax.fori_loop(0, tiles, chunk, [half_of(after_other.at[0], block, groups) for block in range(blocks)])
    for tile in range(tiles):
        for copy in tile_copies(tile, sent, *pairs):
            copy.wait()
    residue_copy.wait()


def swap(value, axis):
    return lax.ppermute(value, axis, [(0, 1), (1, 0)])


def on_device(query_rows, key_rows, value_rows, decay_rate, residue, norm_gain, grad_out):
    tokens, channels = query_rows.shape
    groups = channels // LANES
    half = HALF_MODES * groups
    chips = lax.axis_size(CHIP_AXES)
    cut = half // chips
    natural = shaped(tokens, channels, dtype=bf16)
    dense = shaped(tokens * groups + SUB, LANES)
    modal = shaped(2 * half + groups, LANES)
    halved = shaped(half, LANES)
    two_halves = shaped(2, half, LANES)
    square = shaped(tokens, LANES)
    modal_scratch = pltpu.VMEM((2 * half + groups, LANES), f32)
    natural_scratch = pltpu.VMEM((tokens, channels), bf16)
    token_scratch = pltpu.VMEM((tokens * SUB + SUB, LANES), f32)
    bind = functools.partial

    product, keep, send, shrink, whole, weight, scale_dense, gain = call(
        bind(local_ends, tokens, groups),
        (dense, halved, halved, modal, halved, modal, modal, shaped(1, channels)),
        *[pltpu.with_memory_space_constraint(a, pltpu.HBM) for a in (key_rows, value_rows, decay_rate, residue, norm_gain[None, :])],
        in_specs=[in_hbm] * 5,
        scratch=[
            natural_scratch, natural_scratch, *[pltpu.VMEM((MODES, channels), f32)] * 2, modal_scratch,
            pltpu.SemaphoreType.DMA((2 * CHUNKS + 3,)),
        ],
    )
    whole_cut = whole.reshape(chips, cut, LANES)
    recv = swap(send, "core")
    asked, squared = call(bind(prepare, tokens, groups), (dense, dense), query_rows, grad_out, gain)
    recv, asked, squared = lax.optimization_barrier((recv, asked, squared))
    total = call(chip_total, halved, whole, keep, recv)
    totals = lax.all_to_all(total.reshape(chips, cut, LANES), CHIP_AXES, 0, 0)
    before = call(bind(chip_scan, chips), shaped(chips, cut, LANES), whole_cut, totals)
    chip_state = lax.all_to_all(before, CHIP_AXES, 0, 0).reshape(half, LANES)
    entry_mine, entry_send = call(core_states, (halved, halved), whole, chip_state, keep, recv)
    entry_other = swap(entry_send, "core")

    partial = call(bind(filter_mine, tokens, groups), dense, product, shrink, weight, entry_mine)
    filtered, curved, sums = call(
        bind(filter_other, tokens, groups),
        (dense, dense, shaped(2, tokens)),
        product, shrink, weight, entry_other, partial, asked, squared,
        scratch=[token_scratch, token_scratch],
    )
    other_sums = swap(sums, "tp")

    inverse, slope, grad_filtered, keep, send = call(
        bind(local_adjoint, tokens, groups),
        (square, square, dense, two_halves, two_halves),
        sums, other_sums, asked, curved, product, shrink, scale_dense, entry_mine, entry_other,
    )
    recv = swap(send, "core")
    normed_out, grad_query = call(
        bind(norm_rows, tokens, groups), (natural, natural), inverse, slope, filtered, query_rows, grad_out, gain,
        out_specs=(in_hbm, in_hbm),
        scratch=[natural_scratch, natural_scratch, pltpu.SemaphoreType.DMA((2, tokens // ROWS16))],
    )
    recv, normed_out, grad_query = lax.optimization_barrier((recv, normed_out, grad_query))
    total = call(bind(chip_total_and_sum, half, chips), shaped(chips, 2, cut, LANES), whole, keep, recv)
    totals = lax.all_to_all(total, CHIP_AXES, 0, 0)
    before = call(bind(chip_scan_and_sum, chips), shaped(chips, 2, cut, LANES), whole_cut, totals)
    chip_state = lax.all_to_all(before, CHIP_AXES, 0, 0)
    after_mine, after_send = call(
        bind(core_states_and_sum, half), (two_halves, two_halves), whole, chip_state, keep, recv
    )
    after_other = swap(after_send, "core")

    partial = call(bind(grad_mine, tokens, groups), dense, grad_filtered, shrink, weight, after_mine)
    grad_key, grad_value, grad_residue = call(
        bind(grad_rows, tokens, groups),
        (natural, natural, shaped(MODES, channels)),
        grad_filtered, shrink, weight, after_mine, after_other, partial, key_rows, value_rows,
        out_specs=(in_hbm, in_hbm, in_hbm),
        scratch=[
            modal_scratch, pltpu.VMEM((groups // SUB, ROWS16 * SUB + SUB, LANES), f32), natural_scratch, natural_scratch,
            pltpu.VMEM((MODES, channels), f32), pltpu.SemaphoreType.DMA((2, tokens // ROWS16)), pltpu.SemaphoreType.DMA,
        ],
    )
    return (normed_out, grad_query, grad_key, grad_value, grad_residue)


def solution(mesh):
    devices = mesh.devices
    cut_mesh = Mesh(devices.reshape(CTX_SIZES + (devices.shape[1],)), CTX_AXES + ("tp",))
    token_split = P(CTX_AXES, "tp")
    return jax.shard_map(
        on_device,
        mesh=cut_mesh,
        in_specs=(token_split, token_split, token_split, P(None, "tp"), P(None, "tp"), P("tp"), token_split),
        out_specs=(token_split, token_split, token_split, token_split, P(None, "tp")),
        check_vma=False,
    )
```

time: 108 us -> 94.3 us (0.87)
  local copies, waits for them, and re-layouts: 6.91 us -> 0.34 us
  waiting for transfers between devices: 5.08 us -> 1.52 us
  Pallas kernels: 19 us -> 16.3 us
  other arithmetic: 1.13 us -> 0 us
    unnamed x20 -> x8, local copies, waits for them, and re-layouts: 6.91 us -> 0.34 us
    ppermute x5, waiting for transfers between devices: 5.08 us -> 1.52 us  [swap(): return lax.ppermute(value, axis, [(0, 1), (1, 0)])]
    pallas_call x10 -> x14, Pallas kernels: 19 us -> 16.3 us  [call(): pl.pallas_call(body, out_shape=out_shape, in_specs=in_specs or [in_vmem]...]
    sqrt x1 -> x0, other arithmetic: 1.13 us -> none  [on_device(): in_scale = jnp.sqrt(-jnp.expm1(-2.0 * decay_rate))]
  transfers between devices with their start and end apart: 5 -> 5, of which waited for: 5 -> 2; matrix products, arithmetic and copies ran while one was open for 0% -> 0% of each run, Pallas kernels for 0% -> 5%
where the time goes in v2:
time: 94.3 us; the launch traced here: 94 us
  blocking collectives  62.3 us (66%)
  Pallas kernels  16.3 us (17%)
  starting transfers between devices  12.8 us (14%)
  waiting for transfers between devices  1.52 us (2%)
    all_to_all x1, blocking collectives, on_device(): totals = lax.all_to_all(total.reshape(chips, cut, LANES), CHIP_AXES, 0, 0)  20.2 us
    pallas_call x14, Pallas kernels, call(): pl.pallas_call(body, out_shape=out_shape, in_specs=in_specs or [in_vmem]...  16.3 us
    all_to_all x1, blocking collectives, on_device(): totals = lax.all_to_all(total, CHIP_AXES, 0, 0)  14.5 us
    all_to_all x1, blocking collectives, on_device(): chip_state = lax.all_to_all(before, CHIP_AXES, 0, 0)  14.3 us
    all_to_all x1, blocking collectives, on_device(): chip_state = lax.all_to_all(before, CHIP_AXES, 0, 0).reshape(half, LANES)  13.3 us
    ppermute x5, starting transfers between devices, swap(): return lax.ppermute(value, axis, [(0, 1), (1, 0)])  12.8 us
  transfers between devices with their start and end apart: 5, of which 2 were waited for; matrix products, arithmetic and copies ran while one was open for 0% of the time, Pallas kernels for 5%

profile of v2, /device:TPU:1, one launch (start us, length us, event | category | flops | bytes accessed | tf_op | source)
XLA Modules:
  0.0 94.0 jit_solution(17117800722456103042)
XLA Ops:
  0.6 0.0 copy-start.1
  0.6 0.0 copy-start
  0.7 3.3 %shard_map.110 = (f32[4104,128]{1,0:T(8,128)S(1)}, f32[128,128]{1,0:T(8,128)S(1)}, f32[128,128]{1,0:T(8,128)S(1)}, f32[288,128]{1,0:T(8,128)S(1)}, f32[128,128]{...) custom-call(bf16[128,4096]{1,0:T(8,128)(2,1)} %key.3, ...), custom_call_target="tpu_custom_call" | custom-call | tf_op jit(solution)/shard_map/pallas_call | solution.py:33
  4.0 3.3 %collective-permute-start = (f32[128,128]{1,0:T(8,128)S(1)}, f32[128,128]{1,0:T(8,128)S(1)}, u32[]{:S(2)}, u32[]{:S(2)}) collective-permute-start(f32[128,128]{1,0:T(8,128)S(1)} %get-tuple-element.43), channel_id=1, source_target_pairs={{0,2},{2,0},{1,3},{3,1},{4,6},{6,4},{5,7},{7,5},{8,10},{10,8},{9,1... | collective-permute-start | bytes 196616 | tf_op jit(solution)/shard_map/ppermute | solution.py:445
  7.3 0.0 copy-done.1
  7.3 0.0 copy-done
  7.3 0.7 shard_map.111
  8.0 0.2 collective-permute-done.recv
  8.2 20.2 %all_to_all.20.totals = f32[64,2,128]{2,1,0:T(2,128)S(1)} all-to-all(f32[64,2,128]{2,1,0:T(2,128)S(1)} %bitcast.7), channel_id=1, replica_groups=mesh['x'=4,'yl'=2,'z'=8,'core'=2,'tp'=2] {'x','yl','z'}, dimensions={0} | all-to-all | bytes 131072 | tf_op jit(solution)/shard_map/all_to_all | solution.py:480
  28.4 0.1 shard_map.113
  28.6 13.3 %all_to_all.21 = f32[64,2,128]{2,1,0:T(2,128)S(1)} all-to-all(f32[64,2,128]{2,1,0:T(2,128)S(1)} %shard_map.113), channel_id=1, replica_groups=mesh['x'=4,'yl'=2,'z'=8,'core'=2,'tp'=2] {'x','yl','z'}, dimensions={0} | all-to-all | bytes 131072 | tf_op jit(solution)/shard_map/all_to_all | solution.py:482
  41.9 3.0 %collective-permute-start.1 = (f32[128,128]{1,0:T(8,128)S(1)}, f32[128,128]{1,0:T(8,128)S(1)}, u32[]{:S(2)}, u32[]{:S(2)}) collective-permute-start(f32[128,128]{1,0:T(8,128)S(1)} %get-tuple-element.48), channel_id=1, source_target_pairs={{0,2},{2,0},{1,3},{3,1},{4,6},{6,4},{5,7},{7,5},{8,10},{10,8},{9,1... | collective-permute-start | bytes 196616 | tf_op jit(solution)/shard_map/ppermute | solution.py:445
  44.9 1.1 %shard_map.115.partial = f32[4104,128]{1,0:T(8,128)S(1)} custom-call(f32[4104,128]{1,0:T(8,128)S(1)} %get-tuple-element.38.product, f32[288,128]{1,0:T(8,128)S(1)} %get-tuple-element.39.shrink, f32[288,128]{1,0:T(8,128)S(1)} %get-tuple-element.40.weight, f32[128,128]{1,0:T(8,128)S(1)} %get-tuple-element.49.entry.entry_mine), custom_call_target="tpu_custom_call" | custom-call | tf_op jit(solution)/shard_map/pallas_call | solution.py:33
  46.1 0.0 collective-permute-done.1.entry.entry_other
  46.1 1.9 %shard_map.116 = (f32[4104,128]{1,0:T(8,128)S(1)}, f32[4104,128]{1,0:T(8,128)S(1)}, f32[2,128]{1,0:T(2,128)S(1)}) custom-call(f32[4104,128]{1,0:T(8,128)S(1)} %get-tuple-element.38.product, f32[288,128]{1,0:T(8,128)S(1)} %get-tuple-element.39.shrink, f32[288,128]{1,0:T(8,128)S(1)} %get-tuple-element.40.weight, ...), custom_call_target="tpu_custom_call" | custom-call | tf_op jit(solution)/shard_map/pallas_call | solution.py:33
  48.0 2.7 %collective-permute-start.2 = (f32[2,128]{1,0:T(2,128)S(1)}, f32[2,128]{1,0:T(2,128)S(1)}, u32[]{:S(2)}, u32[]{:S(2)}) collective-permute-start(f32[2,128]{1,0:T(2,128)S(1)} %get-tuple-element.52.sums), channel_id=1, source_target_pairs={{0,1},{1,0},{2,3},{3,2},{4,5},{5,4},{6,7},{7,6},{8,9},{9,8},{10,11... | collective-permute-start | bytes 3080 | tf_op jit(solution)/shard_map/ppermute | solution.py:445
  50.7 1.3 %collective-permute-done.2.other_sums = f32[2,128]{1,0:T(2,128)S(1)} collective-permute-done((f32[2,128]{1,0:T(2,128)S(1)}, f32[2,128]{1,0:T(2,128)S(1)}, u32[]{:S(2)}, u32[]{:S(2)}) %collective-permute-start.2) | collective-permute-done | bytes 1056 | tf_op jit(solution)/shard_map/ppermute | solution.py:445
  52.0 3.1 %shard_map.117 = (f32[128,128]{1,0:T(8,128)S(1)}, f32[128,128]{1,0:T(8,128)S(1)}, f32[4104,128]{1,0:T(8,128)S(1)}, f32[2,128,128]{2,1,0:T(8,128)S(1)}, f32[2,128,128]{2,1,0:T(8,128)S(1)}) custom-call(f32[2,128]{1,0:T(2,128)S(1)} %get-tuple-element.52.sums, f32[2,128]{1,0:T(2,128)S(1)} %collective-permute-done.2.other_sums, ...), custom_call_target="tpu_custom_call" | custom-call | tf_op jit(solution)/shard_map/pallas_call | solution.py:33
  55.1 1.3 %collective-permute-start.3 = (f32[2,128,128]{2,1,0:T(8,128)S(1)}, f32[2,128,128]{2,1,0:T(8,128)S(1)}, u32[]{:S(2)}, u32[]{:S(2)}) collective-permute-start(f32[2,128,128]{2,1,0:T(8,128)S(1)} %get-tuple-element.55), channel_id=1, source_target_pairs={{0,2},{2,0},{1,3},{3,1},{4,6},{6,4},{5,7},{7,5},{8,10},{10,8},{9,1... | collective-permute-start | bytes 393224 | tf_op jit(solution)/shard_map/ppermute | solution.py:445
  56.4 1.8 %shard_map.118 = (bf16[128,4096]{1,0:T(8,128)(2,1)}, bf16[128,4096]{1,0:T(8,128)(2,1)}) custom-call(f32[128,128]{1,0:T(8,128)S(1)} %get-tuple-element.56.inverse, f32[128,128]{1,0:T(8,128)S(1)} %get-tuple-element.57.slope, f32[4104,128]{1,0:T(8,128)S(1)} %get-tuple-element.58.filtered, bf16[128,4096]{1,0:T(8,128)(2,1)S(1)} %copy-done, ...), custom_call_target="tpu_custom_call" | custom-call | tf_op jit(solution)/shard_map/pallas_call | solution.py:33
  58.3 0.0 collective-permute-done.3.recv
  58.3 0.1 shard_map.119
  58.3 14.5 %all_to_all.22.totals = f32[64,2,2,128]{3,2,1,0:T(2,128)S(1)} all-to-all(f32[64,2,2,128]{3,2,1,0:T(2,128)S(1)} %shard_map.119), channel_id=1, replica_groups=mesh['x'=4,'yl'=2,'z'=8,'core'=2,'tp'=2] {'x','yl','z'}, dimensions={0} | all-to-all | bytes 262144 | tf_op jit(solution)/shard_map/all_to_all | solution.py:508
  72.8 0.2 shard_map.120
  73.0 14.3 %all_to_all.23.chip_state = f32[64,2,2,128]{3,2,1,0:T(2,128)S(1)} all-to-all(f32[64,2,2,128]{3,2,1,0:T(2,128)S(1)} %shard_map.120), channel_id=1, replica_groups=mesh['x'=4,'yl'=2,'z'=8,'core'=2,'tp'=2] {'x','yl','z'}, dimensions={0} | all-to-all | bytes 262144 | tf_op jit(solution)/shard_map/all_to_all | solution.py:510
  87.3 0.1 shard_map.121
  87.3 2.4 %collective-permute-start.4 = (f32[2,128,128]{2,1,0:T(8,128)S(1)}, f32[2,128,128]{2,1,0:T(8,128)S(1)}, u32[]{:S(2)}, u32[]{:S(2)}) collective-permute-start(f32[2,128,128]{2,1,0:T(8,128)S(1)} %get-tuple-element.67), channel_id=1, source_target_pairs={{0,2},{2,0},{1,3},{3,1},{4,6},{6,4},{5,7},{7,5},{8,10},{10,8},{9,1... | collective-permute-start | bytes 393224 | tf_op jit(solution)/shard_map/ppermute | solution.py:445
  89.7 0.0 copy-start.2
  89.7 0.0 copy-start.3
  89.7 1.2 %shard_map.122.partial = f32[4104,128]{1,0:T(8,128)S(1)} custom-call(f32[4104,128]{1,0:T(8,128)S(1)} %get-tuple-element.63.grad_filtered, f32[288,128]{1,0:T(8,128)S(1)} %get-tuple-element.39.shrink, f32[288,128]{1,0:T(8,128)S(1)} %get-tuple-element.40.weight, f32[2,128,128]{2,1,0:T(8,128)S(1)} %get-tuple-element.66.after.after_mine), custom_call_target="tpu_custom_call" | custom-call | tf_op jit(solution)/shard_map/pallas_call | solution.py:33
  90.9 0.0 collective-permute-done.4.after_other
  90.9 0.0 copy-done.2
  90.9 0.3 copy-done.3
  91.3 2.8 %shard_map.123 = (bf16[128,4096]{1,0:T(8,128)(2,1)}, bf16[128,4096]{1,0:T(8,128)(2,1)}, f32[8,4096]{1,0:T(8,128)}) custom-call(f32[4104,128]{1,0:T(8,128)S(1)} %get-tuple-element.63.grad_filtered, f32[288,128]{1,0:T(8,128)S(1)} %get-tuple-element.39.shrink, f32[288,128]{1,0:T(8,128)S(1)} %get-tuple-element.40.weight, ...), custom_call_target="tpu_custom_call" | custom-call | tf_op jit(solution)/shard_map/pallas_call | solution.py:33
  (2 shorter events, 0.0 us)
Async XLA Ops:
  0.6 6.7 %copy-start.1 = (bf16[128,4096]{1,0:T(8,128)(2,1)S(1)}, bf16[128,4096]{1,0:T(8,128)(2,1)}, u32[]{:S(2)}) copy-start(bf16[128,4096]{1,0:T(8,128)(2,1)} %grad.3) | copy-start | bytes 3145732
  0.6 6.7 %copy-start = (bf16[128,4096]{1,0:T(8,128)(2,1)S(1)}, bf16[128,4096]{1,0:T(8,128)(2,1)}, u32[]{:S(2)}) copy-start(bf16[128,4096]{1,0:T(8,128)(2,1)} %query.3) | copy-start | bytes 3145732
  4.0 4.2 %collective-permute-start = (f32[128,128]{1,0:T(8,128)S(1)}, f32[128,128]{1,0:T(8,128)S(1)}, u32[]{:S(2)}, u32[]{:S(2)}) collective-permute-start(f32[128,128]{1,0:T(8,128)S(1)} %get-tuple-element.43), channel_id=1, source_target_pairs={{0,2},{2,0},{1,3},{3,1},{4,6},{6,4},{5,7},{7,5},{8,10},{10,8},{9,1... | collective-permute-start | bytes 196616 | tf_op jit(solution)/shard_map/ppermute | solution.py:445
  41.9 4.2 %collective-permute-start.1 = (f32[128,128]{1,0:T(8,128)S(1)}, f32[128,128]{1,0:T(8,128)S(1)}, u32[]{:S(2)}, u32[]{:S(2)}) collective-permute-start(f32[128,128]{1,0:T(8,128)S(1)} %get-tuple-element.48), channel_id=1, source_target_pairs={{0,2},{2,0},{1,3},{3,1},{4,6},{6,4},{5,7},{7,5},{8,10},{10,8},{9,1... | collective-permute-start | bytes 196616 | tf_op jit(solution)/shard_map/ppermute | solution.py:445
  48.0 4.0 %collective-permute-start.2 = (f32[2,128]{1,0:T(2,128)S(1)}, f32[2,128]{1,0:T(2,128)S(1)}, u32[]{:S(2)}, u32[]{:S(2)}) collective-permute-start(f32[2,128]{1,0:T(2,128)S(1)} %get-tuple-element.52.sums), channel_id=1, source_target_pairs={{0,1},{1,0},{2,3},{3,2},{4,5},{5,4},{6,7},{7,6},{8,9},{9,8},{10,11... | collective-permute-start | bytes 3080 | tf_op jit(solution)/shard_map/ppermute | solution.py:445
  55.1 3.1 %collective-permute-start.3 = (f32[2,128,128]{2,1,0:T(8,128)S(1)}, f32[2,128,128]{2,1,0:T(8,128)S(1)}, u32[]{:S(2)}, u32[]{:S(2)}) collective-permute-start(f32[2,128,128]{2,1,0:T(8,128)S(1)} %get-tuple-element.55), channel_id=1, source_target_pairs={{0,2},{2,0},{1,3},{3,1},{4,6},{6,4},{5,7},{7,5},{8,10},{10,8},{9,1... | collective-permute-start | bytes 393224 | tf_op jit(solution)/shard_map/ppermute | solution.py:445
  87.3 3.6 %collective-permute-start.4 = (f32[2,128,128]{2,1,0:T(8,128)S(1)}, f32[2,128,128]{2,1,0:T(8,128)S(1)}, u32[]{:S(2)}, u32[]{:S(2)}) collective-permute-start(f32[2,128,128]{2,1,0:T(8,128)S(1)} %get-tuple-element.67), channel_id=1, source_target_pairs={{0,2},{2,0},{1,3},{3,1},{4,6},{6,4},{5,7},{7,5},{8,10},{10,8},{9,1... | collective-permute-start | bytes 393224 | tf_op jit(solution)/shard_map/ppermute | solution.py:445
  89.7 1.2 %copy-start.2 = (bf16[128,4096]{1,0:T(8,128)(2,1)S(1)}, bf16[128,4096]{1,0:T(8,128)(2,1)}, u32[]{:S(2)}) copy-start(bf16[128,4096]{1,0:T(8,128)(2,1)} %key.3) | copy-start | bytes 3145732
  89.7 1.5 %copy-start.3 = (bf16[128,4096]{1,0:T(8,128)(2,1)S(1)}, bf16[128,4096]{1,0:T(8,128)(2,1)}, u32[]{:S(2)}) copy-start(bf16[128,4096]{1,0:T(8,128)(2,1)} %value.3) | copy-start | bytes 3145732

commit v3 on v2

--- a/solution.py
+++ b/solution.py
@@ -16,7 +16,7 @@
 SUB = 8
 ROWS16 = 16
 UNROLL = 8
-CHUNKS = 4
+CHUNKS = ((0, 2), (2, 8))
 
 CHIP_AXES = ("x", "yl", "z")
 CTX_AXES = CHIP_AXES + ("core",)
@@ -127,18 +127,16 @@
     return [jnp.zeros((SUB, LANES), f32)] * count
 
 
-def local_ends(tokens, groups, key, value, decay, residue, gain, product, keep, send, shrink, whole, weight, scale_dense, gain_in,
-               key_in, value_in, rate_in, residue_in, whole_all, arrived):
-    whole_copies = [
-        pltpu.make_async_copy(source, target, arrived.at[2 * CHUNKS + which])
+def local_ends(tokens, groups, key, value, decay, residue, gain,
+               product, keep, send, shrink, whole, key_in, value_in, rate_in, residue_in, gain_in, whole_all, arrived):
+    rate_copy, *later_copies = [
+        pltpu.make_async_copy(source, target, arrived.at[2 * len(CHUNKS) + which])
         for which, (source, target) in enumerate(((decay, rate_in), (residue, residue_in), (gain, gain_in)))
     ]
-    for copy in whole_copies[:2]:
-        copy.start()
-    some = tokens // CHUNKS
+    rate_copy.start()
     copies = []
-    for chunk in range(CHUNKS):
-        rows = pl.ds(chunk * some, some)
+    for chunk, (begin, end) in enumerate(CHUNKS):
+        rows = pl.ds(begin * tokens // 8, (end - begin) * tokens // 8)
         pair = [
             pltpu.make_async_copy(source.at[rows, :], target.at[rows, :], arrived.at[2 * chunk + which])
             for which, (source, target) in enumerate(((key, key_in), (value, value_in)))
@@ -146,27 +144,24 @@
         for copy in pair:
             copy.start()
         copies.append(pair)
-    whole_copies[2].start()
-    for copy in whole_copies[:2]:
-        copy.wait()
+    for copy in later_copies:
+        copy.start()
+    rate_copy.wait()
     for group in range(groups):
         rows = pl.ds(group, MODES, stride=groups)
         rate = rate_in[:, lanes_of(group)]
-        in_scale = jnp.sqrt(one_minus_exp_of_minus(2.0 * rate))
         shrink[rows, :] = jnp.exp(-rate)
         whole_all[rows, :] = jnp.exp(-rate * tokens)
-        scale_dense[rows, :] = in_scale
-        weight[rows, :] = in_scale * residue_in[:, lanes_of(group)]
     whole[...] = whole_all[my_rows(HALF_MODES * groups), :]
 
     def multiply(first, group):
         store_dense(product, group, first, tokens, tile_of(key_in, first, group) * tile_of(value_in, first, group))
 
-    for chunk in range(CHUNKS):
+    for chunk, (begin, end) in enumerate(CHUNKS):
         for copy in copies[chunk]:
             copy.wait()
-        tiles = some // ROWS16
-        each_tile(chunk * tiles, tiles, groups, multiply)
+        first, some = begin * tokens // 8, (end - begin) * tokens // 8
+        each_tile(first // ROWS16, some // ROWS16, groups, multiply)
         for block in range(groups // SUB):
             ratio = both_halves(shrink, block, groups)
 
@@ -175,11 +170,12 @@
                 return [r * s + row for r, s in zip(ratio, states)]
 
             states = half_of(keep, block, groups) + half_of(send, block, groups) if chunk else zero_states(MODES)
-            states = over_tokens(chunk * some, some, step, states)
+            states = over_tokens(first, some, step, states)
             for mode in range(HALF_MODES):
                 keep[half_rows(block, mode, groups), :] = states[mode]
                 send[half_rows(block, mode, groups), :] = states[HALF_MODES + mode]
-    whole_copies[2].wait()
+    for copy in later_copies:
+        copy.wait()
 
 
 def one_minus_exp_of_minus(value):
@@ -189,7 +185,13 @@
     return jnp.where(value < 0.25, value * series, 1.0 - jnp.exp(-value))
 
 
-def prepare(tokens, groups, query, grad, gain, asked, squared):
+def prepare(tokens, groups, query, grad, gain, decay, residue, asked, squared, weight, scale_dense):
+    for group in range(groups):
+        rows = pl.ds(group, MODES, stride=groups)
+        in_scale = jnp.sqrt(one_minus_exp_of_minus(2.0 * decay[:, lanes_of(group)]))
+        scale_dense[rows, :] = in_scale
+        weight[rows, :] = in_scale * residue[:, lanes_of(group)]
+
     def multiply(first, group):
         rows = tile_of(query, first, group)
         store_dense(asked, group, first, tokens, gain[:, lanes_of(group)] * tile_of(grad, first, group) * rows)
@@ -316,29 +318,18 @@
     ]
 
 
-def norm_rows(tokens, groups, inverse, slope, filtered, query, grad, gain, normed, grad_query, normed_out, grad_out, sent):
-    pairs = ((normed_out, normed), (grad_out, grad_query))
-    tiles = tokens // ROWS16
-
-    def chunk(tile, nothing):
-        first = pl.multiple_of(tile * ROWS16, ROWS16)
+def norm_rows(tokens, groups, inverse, slope, filtered, query, grad, gain, normed, grad_query):
+    def finish(first, group):
         rows = pl.ds(first, ROWS16)
-        for group in range(groups):
-            part = load_dense(filtered, group, first, tokens)
-            gated = tile_of(query, first, group) * part
-            gains = gain[:, lanes_of(group)]
-            scale = inverse[rows, :]
-            normed_out[rows, lanes_of(group)] = (gated * gains * scale).astype(bf16)
-            grad_gated = gains * tile_of(grad, first, group) * scale - gated * slope[rows, :]
-            grad_out[rows, lanes_of(group)] = (grad_gated * part).astype(bf16)
-        for copy in tile_copies(tile, sent, *pairs):
-            copy.start()
-        return nothing
-
-    lax.fori_loop(0, tiles, chunk, 0)
-    for tile in range(tiles):
-        for copy in tile_copies(tile, sent, *pairs):
-            copy.wait()
+        part = load_dense(filtered, group, first, tokens)
+        gated = tile_of(query, first, group) * part
+        gains = gain[:, lanes_of(group)]
+        scale = inverse[rows, :]
+        normed[rows, lanes_of(group)] = (gated * gains * scale).astype(bf16)
+        grad_gated = gains * tile_of(grad, first, group) * scale - gated * slope[rows, :]
+        grad_query[rows, lanes_of(group)] = (grad_gated * part).astype(bf16)
+
+    each_tile(0, tokens // ROWS16, groups, finish)
 
 
 def chip_total_and_sum(half, chips, whole, keep, recv, total):
@@ -397,16 +388,23 @@
         over_tokens(0, tokens, step, [half_of(after.at[0], block, groups) for block in blocks], backward=True)
 
 
-def grad_rows(tokens, groups, grad_filtered, shrink, weight, after_mine, after_other, partial, key, value,
-              grad_key, grad_value, grad_residue, total, dense, key_out, value_out, residue_out, sent, residue_sent):
+def grad_rows(tokens, groups, grad_filtered, shrink, weight, after_mine, after_other, partial, key, value, normed, grad_query,
+              grad_key, grad_value, grad_residue, normed_out, grad_query_out,
+              total, dense, key_out, value_out, residue_out, sent, whole_sent):
     half = HALF_MODES * groups
     core = lax.axis_index("core")
     total[my_rows(half), :] = after_mine[1]
     total[pl.ds(pl.multiple_of((1 - core) * half, half), half), :] = after_other[1]
     for group in range(groups):
         residue_out[:, lanes_of(group)] = total[pl.ds(group, MODES, stride=groups), :]
-    residue_copy = pltpu.make_async_copy(residue_out, grad_residue, residue_sent)
-    residue_copy.start()
+    whole_copies = [
+        pltpu.make_async_copy(source, target, whole_sent.at[which])
+        for which, (source, target) in enumerate(
+            ((normed, normed_out), (grad_query, grad_query_out), (residue_out, grad_residue))
+        )
+    ]
+    for copy in whole_copies:
+        copy.start()
     blocks = groups // SUB
     tiles = tokens // ROWS16
 
@@ -438,7 +436,8 @@
     for tile in range(tiles):
         for copy in tile_copies(tile, sent, *pairs):
             copy.wait()
-    residue_copy.wait()
+    for copy in whole_copies:
+        copy.wait()
 
 
 def swap(value, axis):
@@ -452,6 +451,7 @@
     chips = lax.axis_size(CHIP_AXES)
     cut = half // chips
     natural = shaped(tokens, channels, dtype=bf16)
+    rates = shaped(MODES, channels)
     dense = shaped(tokens * groups + SUB, LANES)
     modal = shaped(2 * half + groups, LANES)
     halved = shaped(half, LANES)
@@ -462,20 +462,20 @@
     token_scratch = pltpu.VMEM((tokens * SUB + SUB, LANES), f32)
     bind = functools.partial
 
-    product, keep, send, shrink, whole, weight, scale_dense, gain = call(
+    inputs = (key_rows, value_rows, decay_rate, residue, norm_gain[None, :])
+    product, keep, send, shrink, whole, key_near, value_near, rate_near, residue_near, gain = call(
         bind(local_ends, tokens, groups),
-        (dense, halved, halved, modal, halved, modal, modal, shaped(1, channels)),
-        *[pltpu.with_memory_space_constraint(a, pltpu.HBM) for a in (key_rows, value_rows, decay_rate, residue, norm_gain[None, :])],
-        in_specs=[in_hbm] * 5,
-        scratch=[
-            natural_scratch, natural_scratch, *[pltpu.VMEM((MODES, channels), f32)] * 2, modal_scratch,
-            pltpu.SemaphoreType.DMA((2 * CHUNKS + 3,)),
-        ],
+        (dense, halved, halved, modal, halved, natural, natural, rates, rates, shaped(1, channels)),
+        *[pltpu.with_memory_space_constraint(array, pltpu.HBM) for array in inputs],
+        in_specs=[in_hbm] * len(inputs),
+        scratch=[modal_scratch, pltpu.SemaphoreType.DMA((2 * len(CHUNKS) + 3,))],
     )
     whole_cut = whole.reshape(chips, cut, LANES)
     recv = swap(send, "core")
-    asked, squared = call(bind(prepare, tokens, groups), (dense, dense), query_rows, grad_out, gain)
-    recv, asked, squared = lax.optimization_barrier((recv, asked, squared))
+    asked, squared, weight, scale_dense = call(
+        bind(prepare, tokens, groups), (dense, dense, modal, modal), query_rows, grad_out, gain, rate_near, residue_near
+    )
+    recv, asked = lax.optimization_barrier((recv, asked))
     total = call(chip_total, halved, whole, keep, recv)
     totals = lax.all_to_all(total.reshape(chips, cut, LANES), CHIP_AXES, 0, 0)
     before = call(bind(chip_scan, chips), shaped(chips, cut, LANES), whole_cut, totals)
@@ -498,12 +498,10 @@
         sums, other_sums, asked, curved, product, shrink, scale_dense, entry_mine, entry_other,
     )
     recv = swap(send, "core")
-    normed_out, grad_query = call(
-        bind(norm_rows, tokens, groups), (natural, natural), inverse, slope, filtered, query_rows, grad_out, gain,
-        out_specs=(in_hbm, in_hbm),
-        scratch=[natural_scratch, natural_scratch, pltpu.SemaphoreType.DMA((2, tokens // ROWS16))],
-    )
-    recv, normed_out, grad_query = lax.optimization_barrier((recv, normed_out, grad_query))
+    normed_near, grad_query_near = call(
+        bind(norm_rows, tokens, groups), (natural, natural), inverse, slope, filtered, query_rows, grad_out, gain
+    )
+    recv, normed_near, grad_query_near = lax.optimization_barrier((recv, normed_near, grad_query_near))
     total = call(bind(chip_total_and_sum, half, chips), shaped(chips, 2, cut, LANES), whole, keep, recv)
     totals = lax.all_to_all(total, CHIP_AXES, 0, 0)
     before = call(bind(chip_scan_and_sum, chips), shaped(chips, 2, cut, LANES), whole_cut, totals)
@@ -514,14 +512,14 @@
     after_other = swap(after_send, "core")
 
     partial = call(bind(grad_mine, tokens, groups), dense, grad_filtered, shrink, weight, after_mine)
-    grad_key, grad_value, grad_residue = call(
+    grad_key, grad_value, grad_residue, normed_out, grad_query = call(
         bind(grad_rows, tokens, groups),
-        (natural, natural, shaped(MODES, channels)),
-        grad_filtered, shrink, weight, after_mine, after_other, partial, key_rows, value_rows,
-        out_specs=(in_hbm, in_hbm, in_hbm),
+        (natural, natural, rates, natural, natural),
+        grad_filtered, shrink, weight, after_mine, after_other, partial, key_near, value_near, normed_near, grad_query_near,
+        out_specs=(in_hbm,) * 5,
         scratch=[
             modal_scratch, pltpu.VMEM((groups // SUB, ROWS16 * SUB + SUB, LANES), f32), natural_scratch, natural_scratch,
-            pltpu.VMEM((MODES, channels), f32), pltpu.SemaphoreType.DMA((2, tokens // ROWS16)), pltpu.SemaphoreType.DMA,
+            pltpu.VMEM((MODES, channels), f32), pltpu.SemaphoreType.DMA((2, tokens // ROWS16)), pltpu.SemaphoreType.DMA((3,)),
         ],
     )
     return (normed_out, grad_query, grad_key, grad_value, grad_residue)

time: 94.3 us -> 92.8 us (0.984)
  transfers between devices with their start and end apart: 5 -> 5, of which waited for: 2 -> 1; matrix products, arithmetic and copies ran while one was open for 0% -> 0% of each run, Pallas kernels for 5% -> 5%
where the time goes in v3:
time: 92.8 us; the launch traced here: 92.6 us
  blocking collectives  62.1 us (67%)
  Pallas kernels  15.5 us (17%)
  starting transfers between devices  12.9 us (14%)
  waiting for transfers between devices  1.33 us (1%)
    all_to_all x1, blocking collectives, on_device(): totals = lax.all_to_all(total.reshape(chips, cut, LANES), CHIP_AXES, 0, 0)  20.2 us
    pallas_call x14, Pallas kernels, call(): pl.pallas_call(body, out_shape=out_shape, in_specs=in_specs or [in_vmem]...  15.5 us
    all_to_all x1, blocking collectives, on_device(): chip_state = lax.all_to_all(before, CHIP_AXES, 0, 0)  14.4 us
    all_to_all x1, blocking collectives, on_device(): totals = lax.all_to_all(total, CHIP_AXES, 0, 0)  14.2 us
    all_to_all x1, blocking collectives, on_device(): chip_state = lax.all_to_all(before, CHIP_AXES, 0, 0).reshape(half, LANES)  13.3 us
    ppermute x5, starting transfers between devices, swap(): return lax.ppermute(value, axis, [(0, 1), (1, 0)])  12.9 us
  transfers between devices with their start and end apart: 5, of which 1 were waited for; matrix products, arithmetic and copies ran while one was open for 0% of the time, Pallas kernels for 5%

profile of v3, /device:TPU:1, one launch (start us, length us, event | category | flops | bytes accessed | tf_op | source)
XLA Modules:
  0.0 92.6 jit_solution(12262912204749924674)
XLA Ops:
  0.6 0.0 copy-start.1
  0.6 0.0 copy-start
  0.7 3.0 %shard_map.110 = (f32[4104,128]{1,0:T(8,128)S(1)}, f32[128,128]{1,0:T(8,128)S(1)}, f32[128,128]{1,0:T(8,128)S(1)}, f32[288,128]{1,0:T(8,128)S(1)}, f32[128,128]{...) custom-call(bf16[128,4096]{1,0:T(8,128)(2,1)} %key.1, ...), custom_call_target="tpu_custom_call" | custom-call | tf_op jit(solution)/shard_map/pallas_call | solution.py:33
  3.7 3.3 %collective-permute-start = (f32[128,128]{1,0:T(8,128)S(1)}, f32[128,128]{1,0:T(8,128)S(1)}, u32[]{:S(2)}, u32[]{:S(2)}) collective-permute-start(f32[128,128]{1,0:T(8,128)S(1)} %get-tuple-element.51), channel_id=1, source_target_pairs={{0,2},{2,0},{1,3},{3,1},{4,6},{6,4},{5,7},{7,5},{8,10},{10,8},{9,1... | collective-permute-start | bytes 196616 | tf_op jit(solution)/shard_map/ppermute | solution.py:444
  7.0 0.0 copy-done.1
  7.0 0.0 copy-done
  7.0 1.0 %shard_map.111 = (f32[4104,128]{1,0:T(8,128)S(1)}, f32[4104,128]{1,0:T(8,128)S(1)}, f32[288,128]{1,0:T(8,128)S(1)}, f32[288,128]{1,0:T(8,128)S(1)}) custom-call(bf16[128,4096]{1,0:T(8,128)(2,1)S(1)} %copy-done, bf16[128,4096]{1,0:T(8,128)(2,1)S(1)} %copy-done.1, f32[1,4096]{1,0:T(1,128)S(1)} %get-tuple-element.45.gain, ...), custom_call_target="tpu_custom_call" | custom-call | tf_op jit(solution)/shard_map/pallas_call | solution.py:33
  8.0 0.0 collective-permute-done.recv
  8.0 20.2 %all_to_all.20.totals = f32[64,2,128]{2,1,0:T(2,128)S(1)} all-to-all(f32[64,2,128]{2,1,0:T(2,128)S(1)} %bitcast.7), channel_id=1, replica_groups=mesh['x'=4,'yl'=2,'z'=8,'core'=2,'tp'=2] {'x','yl','z'}, dimensions={0} | all-to-all | bytes 131072 | tf_op jit(solution)/shard_map/all_to_all | solution.py:480
  28.2 0.1 shard_map.113
  28.4 13.3 %all_to_all.21 = f32[64,2,128]{2,1,0:T(2,128)S(1)} all-to-all(f32[64,2,128]{2,1,0:T(2,128)S(1)} %shard_map.113), channel_id=1, replica_groups=mesh['x'=4,'yl'=2,'z'=8,'core'=2,'tp'=2] {'x','yl','z'}, dimensions={0} | all-to-all | bytes 131072 | tf_op jit(solution)/shard_map/all_to_all | solution.py:482
  41.7 2.9 %collective-permute-start.1 = (f32[128,128]{1,0:T(8,128)S(1)}, f32[128,128]{1,0:T(8,128)S(1)}, u32[]{:S(2)}, u32[]{:S(2)}) collective-permute-start(f32[128,128]{1,0:T(8,128)S(1)} %get-tuple-element.54), channel_id=1, source_target_pairs={{0,2},{2,0},{1,3},{3,1},{4,6},{6,4},{5,7},{7,5},{8,10},{10,8},{9,1... | collective-permute-start | bytes 196616 | tf_op jit(solution)/shard_map/ppermute | solution.py:444
  44.6 1.1 %shard_map.115.partial = f32[4104,128]{1,0:T(8,128)S(1)} custom-call(f32[4104,128]{1,0:T(8,128)S(1)} %get-tuple-element.43.product, f32[288,128]{1,0:T(8,128)S(1)} %get-tuple-element.44.shrink, f32[288,128]{1,0:T(8,128)S(1)} %get-tuple-element.48.weight, f32[128,128]{1,0:T(8,128)S(1)} %get-tuple-element.55.entry.entry_mine), custom_call_target="tpu_custom_call" | custom-call | tf_op jit(solution)/shard_map/pallas_call | solution.py:33
  45.8 0.0 collective-permute-done.1.entry.entry_other
  45.8 1.9 %shard_map.116 = (f32[4104,128]{1,0:T(8,128)S(1)}, f32[4104,128]{1,0:T(8,128)S(1)}, f32[2,128]{1,0:T(2,128)S(1)}) custom-call(f32[4104,128]{1,0:T(8,128)S(1)} %get-tuple-element.43.product, f32[288,128]{1,0:T(8,128)S(1)} %get-tuple-element.44.shrink, f32[288,128]{1,0:T(8,128)S(1)} %get-tuple-element.48.weight, ...), custom_call_target="tpu_custom_call" | custom-call | tf_op jit(solution)/shard_map/pallas_call | solution.py:33
  47.7 2.7 %collective-permute-start.2 = (f32[2,128]{1,0:T(2,128)S(1)}, f32[2,128]{1,0:T(2,128)S(1)}, u32[]{:S(2)}, u32[]{:S(2)}) collective-permute-start(f32[2,128]{1,0:T(2,128)S(1)} %get-tuple-element.58.sums), channel_id=1, source_target_pairs={{0,1},{1,0},{2,3},{3,2},{4,5},{5,4},{6,7},{7,6},{8,9},{9,8},{10,11... | collective-permute-start | bytes 3080 | tf_op jit(solution)/shard_map/ppermute | solution.py:444
  50.4 1.3 %collective-permute-done.2.other_sums = f32[2,128]{1,0:T(2,128)S(1)} collective-permute-done((f32[2,128]{1,0:T(2,128)S(1)}, f32[2,128]{1,0:T(2,128)S(1)}, u32[]{:S(2)}, u32[]{:S(2)}) %collective-permute-start.2) | collective-permute-done | bytes 1056 | tf_op jit(solution)/shard_map/ppermute | solution.py:444
  51.7 3.1 %shard_map.117 = (f32[128,128]{1,0:T(8,128)S(1)}, f32[128,128]{1,0:T(8,128)S(1)}, f32[4104,128]{1,0:T(8,128)S(1)}, f32[2,128,128]{2,1,0:T(8,128)S(1)}, f32[2,128,128]{2,1,0:T(8,128)S(1)}) custom-call(f32[2,128]{1,0:T(2,128)S(1)} %get-tuple-element.58.sums, f32[2,128]{1,0:T(2,128)S(1)} %collective-permute-done.2.other_sums, ...), custom_call_target="tpu_custom_call" | custom-call | tf_op jit(solution)/shard_map/pallas_call | solution.py:33
  54.8 1.3 %collective-permute-start.3 = (f32[2,128,128]{2,1,0:T(8,128)S(1)}, f32[2,128,128]{2,1,0:T(8,128)S(1)}, u32[]{:S(2)}, u32[]{:S(2)}) collective-permute-start(f32[2,128,128]{2,1,0:T(8,128)S(1)} %get-tuple-element.63), channel_id=1, source_target_pairs={{0,2},{2,0},{1,3},{3,1},{4,6},{6,4},{5,7},{7,5},{8,10},{10,8},{9,1... | collective-permute-start | bytes 393224 | tf_op jit(solution)/shard_map/ppermute | solution.py:444
  56.1 1.0 %shard_map.118 = (bf16[128,4096]{1,0:T(8,128)(2,1)S(1)}, bf16[128,4096]{1,0:T(8,128)(2,1)S(1)}) custom-call(f32[128,128]{1,0:T(8,128)S(1)} %get-tuple-element.64.inverse, f32[128,128]{1,0:T(8,128)S(1)} %get-tuple-element.65.slope, f32[4104,128]{1,0:T(8,128)S(1)} %get-tuple-element.66.filtered, bf16[128,4096]{1,0:T(8,128)(2,1)S(1)} %copy-done, ...), custom_call_target="tpu_custom_call" | custom-call | tf_op jit(solution)/shard_map/pallas_call | solution.py:33
  57.1 0.0 collective-permute-done.3.recv
  57.1 0.1 shard_map.119
  57.2 14.2 %all_to_all.22.totals = f32[64,2,2,128]{3,2,1,0:T(2,128)S(1)} all-to-all(f32[64,2,2,128]{3,2,1,0:T(2,128)S(1)} %shard_map.119), channel_id=1, replica_groups=mesh['x'=4,'yl'=2,'z'=8,'core'=2,'tp'=2] {'x','yl','z'}, dimensions={0} | all-to-all | bytes 262144 | tf_op jit(solution)/shard_map/all_to_all | solution.py:506
  71.3 0.2 shard_map.120
  71.5 14.4 %all_to_all.23.chip_state = f32[64,2,2,128]{3,2,1,0:T(2,128)S(1)} all-to-all(f32[64,2,2,128]{3,2,1,0:T(2,128)S(1)} %shard_map.120), channel_id=1, replica_groups=mesh['x'=4,'yl'=2,'z'=8,'core'=2,'tp'=2] {'x','yl','z'}, dimensions={0} | all-to-all | bytes 262144 | tf_op jit(solution)/shard_map/all_to_all | solution.py:508
  85.9 0.1 shard_map.121
  85.9 2.6 %collective-permute-start.4 = (f32[2,128,128]{2,1,0:T(8,128)S(1)}, f32[2,128,128]{2,1,0:T(8,128)S(1)}, u32[]{:S(2)}, u32[]{:S(2)}) collective-permute-start(f32[2,128,128]{2,1,0:T(8,128)S(1)} %get-tuple-element.71), channel_id=1, source_target_pairs={{0,2},{2,0},{1,3},{3,1},{4,6},{6,4},{5,7},{7,5},{8,10},{10,8},{9,1... | collective-permute-start | bytes 393224 | tf_op jit(solution)/shard_map/ppermute | solution.py:444
  88.6 1.2 %shard_map.122.partial = f32[4104,128]{1,0:T(8,128)S(1)} custom-call(f32[4104,128]{1,0:T(8,128)S(1)} %get-tuple-element.61.grad_filtered, f32[288,128]{1,0:T(8,128)S(1)} %get-tuple-element.44.shrink, f32[288,128]{1,0:T(8,128)S(1)} %get-tuple-element.48.weight, f32[2,128,128]{2,1,0:T(8,128)S(1)} %get-tuple-element.70.after.after_mine), custom_call_target="tpu_custom_call" | custom-call | tf_op jit(solution)/shard_map/pallas_call | solution.py:33
  89.8 0.0 collective-permute-done.4.after_other
  89.8 2.8 %shard_map.123 = (bf16[128,4096]{1,0:T(8,128)(2,1)}, bf16[128,4096]{1,0:T(8,128)(2,1)}, f32[8,4096]{1,0:T(8,128)}, bf16[128,4096]{1,0:T(8,128)(2,1)}, bf16[128,4096]{1,0:T(8,128)(2,1)}) custom-call(f32[4104,128]{1,0:T(8,128)S(1)} %get-tuple-element.61.grad_filtered, f32[288,128]{1,0:T(8,128)S(1)} %get-tuple-element.44.shrink, ...), custom_call_target="tpu_custom_call" | custom-call | tf_op jit(solution)/shard_map/pallas_call | solution.py:33
  (2 shorter events, 0.1 us)
Async XLA Ops:
  0.6 6.3 %copy-start.1 = (bf16[128,4096]{1,0:T(8,128)(2,1)S(1)}, bf16[128,4096]{1,0:T(8,128)(2,1)}, u32[]{:S(2)}) copy-start(bf16[128,4096]{1,0:T(8,128)(2,1)} %grad.3) | copy-start | bytes 3145732
  0.6 6.3 %copy-start = (bf16[128,4096]{1,0:T(8,128)(2,1)S(1)}, bf16[128,4096]{1,0:T(8,128)(2,1)}, u32[]{:S(2)}) copy-start(bf16[128,4096]{1,0:T(8,128)(2,1)} %query.3) | copy-start | bytes 3145732
  3.7 4.3 %collective-permute-start = (f32[128,128]{1,0:T(8,128)S(1)}, f32[128,128]{1,0:T(8,128)S(1)}, u32[]{:S(2)}, u32[]{:S(2)}) collective-permute-start(f32[128,128]{1,0:T(8,128)S(1)} %get-tuple-element.51), channel_id=1, source_target_pairs={{0,2},{2,0},{1,3},{3,1},{4,6},{6,4},{5,7},{7,5},{8,10},{10,8},{9,1... | collective-permute-start | bytes 196616 | tf_op jit(solution)/shard_map/ppermute | solution.py:444
  41.7 4.1 %collective-permute-start.1 = (f32[128,128]{1,0:T(8,128)S(1)}, f32[128,128]{1,0:T(8,128)S(1)}, u32[]{:S(2)}, u32[]{:S(2)}) collective-permute-start(f32[128,128]{1,0:T(8,128)S(1)} %get-tuple-element.54), channel_id=1, source_target_pairs={{0,2},{2,0},{1,3},{3,1},{4,6},{6,4},{5,7},{7,5},{8,10},{10,8},{9,1... | collective-permute-start | bytes 196616 | tf_op jit(solution)/shard_map/ppermute | solution.py:444
  47.7 4.0 %collective-permute-start.2 = (f32[2,128]{1,0:T(2,128)S(1)}, f32[2,128]{1,0:T(2,128)S(1)}, u32[]{:S(2)}, u32[]{:S(2)}) collective-permute-start(f32[2,128]{1,0:T(2,128)S(1)} %get-tuple-element.58.sums), channel_id=1, source_target_pairs={{0,1},{1,0},{2,3},{3,2},{4,5},{5,4},{6,7},{7,6},{8,9},{9,8},{10,11... | collective-permute-start | bytes 3080 | tf_op jit(solution)/shard_map/ppermute | solution.py:444
  54.8 2.3 %collective-permute-start.3 = (f32[2,128,128]{2,1,0:T(8,128)S(1)}, f32[2,128,128]{2,1,0:T(8,128)S(1)}, u32[]{:S(2)}, u32[]{:S(2)}) collective-permute-start(f32[2,128,128]{2,1,0:T(8,128)S(1)} %get-tuple-element.63), channel_id=1, source_target_pairs={{0,2},{2,0},{1,3},{3,1},{4,6},{6,4},{5,7},{7,5},{8,10},{10,8},{9,1... | collective-permute-start | bytes 393224 | tf_op jit(solution)/shard_map/ppermute | solution.py:444
  85.9 3.8 %collective-permute-start.4 = (f32[2,128,128]{2,1,0:T(8,128)S(1)}, f32[2,128,128]{2,1,0:T(8,128)S(1)}, u32[]{:S(2)}, u32[]{:S(2)}) collective-permute-start(f32[2,128,128]{2,1,0:T(8,128)S(1)} %get-tuple-element.71), channel_id=1, source_target_pairs={{0,2},{2,0},{1,3},{3,1},{4,6},{6,4},{5,7},{7,5},{8,10},{10,8},{9,1... | collective-permute-start | bytes 393224 | tf_op jit(solution)/shard_map/ppermute | solution.py:444

commit v4 on v3

--- a/solution.py
+++ b/solution.py
@@ -15,7 +15,7 @@
 LANES = 128
 SUB = 8
 ROWS16 = 16
-UNROLL = 8
+STEP = 4
 CHUNKS = ((0, 2), (2, 8))
 
 CHIP_AXES = ("x", "yl", "z")
@@ -109,14 +109,46 @@
     return terms[0]
 
 
-def over_tokens(first, count, step, carried, backward=False):
+def over_steps(first, count, together, body, carried, backward=False):
     def several(turn, carried):
-        for inner in range(UNROLL):
-            at = turn * UNROLL + inner
-            carried = step(first + (count - 1 - at if backward else at), carried)
+        for inner in range(together):
+            at = turn * together + inner
+            carried = body(first + (count - 1 - at if backward else at), carried)
         return carried
 
-    return lax.fori_loop(0, count // UNROLL, several, carried)
+    return lax.fori_loop(0, count // together, several, carried)
+
+
+def step_rows(block, step, mode, steps):
+    return pl.ds(pl.multiple_of(((block * steps + step) * MODES + mode) * SUB, SUB), SUB)
+
+
+def boundary(ref, block, step, steps, mine):
+    modes = range(HALF_MODES) if mine else range(HALF_MODES, MODES)
+    return [ref[step_rows(block, step, mode, steps), :] for mode in modes]
+
+
+def put_boundary(ref, block, step, steps, states):
+    for mode in range(MODES):
+        ref[step_rows(block, step, mode, steps), :] = states[mode]
+
+
+def powers(ratio, factor):
+    rising, passed = [factor], ratio
+    for turn in range(STEP):
+        rising.append([f * r for f, r in zip(rising[-1], ratio)])
+        if turn:
+            passed = [p * r for p, r in zip(passed, ratio)]
+    return rising[1:], passed
+
+
+def taps(shrink, weight, block, groups):
+    ratio, now = both_halves(shrink, block, groups), both_halves(weight, block, groups)
+    result = []
+    for _ in range(STEP):
+        result.append(tree_sum(now))
+        now = [n * r for n, r in zip(now, ratio)]
+    return result
 
 
 def token_row(block, token, tokens):
@@ -128,7 +160,7 @@
 
 
 def local_ends(tokens, groups, key, value, decay, residue, gain,
-               product, keep, send, shrink, whole, key_in, value_in, rate_in, residue_in, gain_in, whole_all, arrived):
+               product, local_states, keep, send, shrink, whole, key_in, value_in, rate_in, residue_in, gain_in, whole_all, arrived):
     rate_copy, *later_copies = [
         pltpu.make_async_copy(source, target, arrived.at[2 * len(CHUNKS) + which])
         for which, (source, target) in enumerate(((decay, rate_in), (residue, residue_in), (gain, gain_in)))
@@ -165,12 +197,15 @@
         for block in range(groups // SUB):
             ratio = both_halves(shrink, block, groups)
 
-            def step(token, states):
-                row = product[token_row(block, token, tokens), :]
-                return [r * s + row for r, s in zip(ratio, states)]
+            def advance(step, states):
+                put_boundary(local_states, block, step, tokens // STEP, states)
+                for inner in range(STEP):
+                    row = product[token_row(block, step * STEP + inner, tokens), :]
+                    states = [r * s + row for r, s in zip(ratio, states)]
+                return states
 
             states = half_of(keep, block, groups) + half_of(send, block, groups) if chunk else zero_states(MODES)
-            states = over_tokens(first, some, step, states)
+            states = over_steps(first // STEP, some // STEP, 4, advance, states)
             for mode in range(HALF_MODES):
                 keep[half_rows(block, mode, groups), :] = states[mode]
                 send[half_rows(block, mode, groups), :] = states[HALF_MODES + mode]
@@ -228,60 +263,70 @@
     other[...] = jnp.where(mine_is_farther, second, first)
 
 
-def filter_mine(tokens, groups, product, shrink, weight, entry, partial):
-    for pair in range(0, groups // SUB, 2):
-        blocks = (pair, pair + 1)
-        ratio = [core_half(shrink, block, groups, True) for block in blocks]
-        factor = [core_half(weight, block, groups, True) for block in blocks]
-
-        def step(token, states):
-            result = []
-            for which, block in enumerate(blocks):
+def filter_mine(tokens, groups, product, local_states, shrink, weight, entry, partial):
+    steps = tokens // STEP
+    for block in range(groups // SUB):
+        rising, passed = powers(core_half(shrink, block, groups, True), core_half(weight, block, groups, True))
+        tap = taps(shrink, weight, block, groups)
+
+        def advance(step, entering):
+            states = [s + e for s, e in zip(boundary(local_states, block, step, steps, True), entering)]
+            rows = []
+            for inner in range(STEP):
+                at = token_row(block, step * STEP + inner, tokens)
+                rows.append(product[at, :])
+                own = [tap[inner - back] * rows[back] for back in range(inner + 1)]
+                partial[at, :] = tree_sum([w * s for w, s in zip(rising[inner], states)] + own)
+            return [p * e for p, e in zip(passed, entering)]
+
+        over_steps(0, steps, 4, advance, half_of(entry, block, groups))
+
+
+def filter_other(tokens, groups, local_states, shrink, weight, entry, partial, asked, squared, filtered, curved, sums, squares, dots):
+    steps = tokens // STEP
+    for block in range(groups // SUB):
+        rising, passed = powers(core_half(shrink, block, groups, False), core_half(weight, block, groups, False))
+
+        def advance(step, entering):
+            states = [s + e for s, e in zip(boundary(local_states, block, step, steps, False), entering)]
+            for inner in range(STEP):
+                token = step * STEP + inner
                 at = token_row(block, token, tokens)
-                row = product[at, :]
-                now = [r * s + row for r, s in zip(ratio[which], states[which])]
-                partial[at, :] = tree_sum([w * s for w, s in zip(factor[which], now)])
-                result.append(now)
-            return result
-
-        over_tokens(0, tokens, step, [half_of(entry, block, groups) for block in blocks])
-
-
-def filter_other(tokens, groups, product, shrink, weight, entry, partial, asked, squared, filtered, curved, sums, squares, dots):
-    for pair in range(0, groups // SUB, 2):
-        blocks = (pair, pair + 1)
-        ratio = [core_half(shrink, block, groups, False) for block in blocks]
-        factor = [core_half(weight, block, groups, False) for block in blocks]
-
-        def step(token, states):
-            result, square_terms, dot_terms = [], [], []
-            for which, block in enumerate(blocks):
-                at = token_row(block, token, tokens)
-                row = product[at, :]
-                now = [r * s + row for r, s in zip(ratio[which], states[which])]
-                value = partial[at, :] + tree_sum([w * s for w, s in zip(factor[which], now)])
+                value = tree_sum([w * s for w, s in zip(rising[inner], states)]) + partial[at, :]
                 bent = squared[at, :] * value
                 filtered[at, :] = value
                 curved[at, :] = bent
-                square_terms.append(bent * value)
-                dot_terms.append(asked[at, :] * value)
-                result.append(now)
-            rows = token_row(0, token, tokens)
-            if pair:
-                square_terms.append(squares[rows, :])
-                dot_terms.append(dots[rows, :])
-            squares[rows, :] = tree_sum(square_terms)
-            dots[rows, :] = tree_sum(dot_terms)
-            return result
-
-        over_tokens(0, tokens, step, [half_of(entry, block, groups) for block in blocks])
+                rows = token_row(0, token, tokens)
+                square_term, dot_term = bent * value, asked[at, :] * value
+                squares[rows, :] = square_term + squares[rows, :] if block else square_term
+                dots[rows, :] = dot_term + dots[rows, :] if block else dot_term
+            return [p * e for p, e in zip(passed, entering)]
+
+        over_steps(0, steps, 4, advance, half_of(entry, block, groups))
     for line, ref in enumerate((squares, dots)):
         per_token = tree_sum([ref[pl.ds(shift, tokens, stride=SUB), :] for shift in range(SUB)])
         sums[line : line + 1, :] = jnp.sum(per_token.T, axis=0, keepdims=True)
 
 
-def local_adjoint(tokens, groups, sums, other_sums, asked, curved, product, shrink, scale_dense, entry_mine, entry_other,
-                  inverse, slope, grad_filtered, keep, send):
+def step_sums(tokens, groups, product, shrink, sums):
+    steps = tokens // STEP
+    for block in range(groups // SUB):
+        ratio = both_halves(shrink, block, groups)
+
+        def gather(step, nothing):
+            rows = [product[token_row(block, step * STEP + inner, tokens), :] for inner in range(STEP)]
+            total = [r * rows[0] for r in ratio]
+            for row in rows[1:]:
+                total = [r * (row + t) for r, t in zip(ratio, total)]
+            put_boundary(sums, block, step, steps, total)
+            return nothing
+
+        over_steps(0, steps, 4, gather, 0)
+
+
+def local_adjoint(tokens, groups, sums, other_sums, asked, curved, product, product_sums, shrink, scale_dense, entry_mine, entry_other,
+                  inverse, slope, grad_filtered, local_adjoints, keep, send):
+    steps = tokens // STEP
     both = sums[...] + other_sums[...]
     rms = jnp.sqrt(both[0:1] / D + norm_eps)
     inverse[...] = jnp.broadcast_to(1.0 / rms, (LANES, tokens)).T
@@ -289,18 +334,32 @@
     for block in range(groups // SUB):
         ratio = both_halves(shrink, block, groups)
 
-        def step(token, carried):
-            states, terms = carried
-            at = token_row(block, token, tokens)
-            now = pl.ds(token, 1)
-            row = inverse[now, :] * asked[at, :] - slope[now, :] * curved[at, :]
-            grad_filtered[at, :] = row
-            put_in = product[at, :]
-            states = [r * s + row for r, s in zip(ratio, states)]
-            terms = [q + put_in * s for q, s in zip(terms, states)]
-            return states, terms
-
-        states, terms = over_tokens(0, tokens, step, (zero_states(MODES), zero_states(MODES)), backward=True)
+        def advance(step, carried):
+            states, terms, shared = carried
+            put_boundary(local_adjoints, block, step, steps, states)
+            along = boundary(product_sums, block, step, steps, True) + boundary(product_sums, block, step, steps, False)
+            terms = [q + a * s for q, a, s in zip(terms, along, states)]
+            grads = [None] * STEP
+            for inner in range(STEP - 1, -1, -1):
+                token = step * STEP + inner
+                at = token_row(block, token, tokens)
+                now = pl.ds(token, 1)
+                grads[inner] = inverse[now, :] * asked[at, :] - slope[now, :] * curved[at, :]
+                grad_filtered[at, :] = grads[inner]
+                states = [r * s + grads[inner] for r, s in zip(ratio, states)]
+                put_in = product[at, :]
+                shared = [
+                    c + put_in * grads[inner + apart] if inner + apart < STEP else c for apart, c in enumerate(shared)
+                ]
+            return states, terms, shared
+
+        start = (zero_states(MODES), zero_states(MODES), zero_states(STEP))
+        states, terms, shared = over_steps(0, steps, 2, advance, start, backward=True)
+        for mode in range(MODES):
+            near = shared[STEP - 1]
+            for part in shared[STEP - 2 :: -1]:
+                near = part + ratio[mode] * near
+            terms[mode] = terms[mode] + near
         entry = half_of(entry_mine, block, groups) + half_of(entry_other, block, groups)
         scale = both_halves(scale_dense, block, groups)
         terms = [i * (q + r * s * e) for i, q, r, s, e in zip(scale, terms, ratio, states, entry)]
@@ -369,28 +428,28 @@
     other[1] = summed
 
 
-def grad_mine(tokens, groups, grad_filtered, shrink, weight, after, partial):
-    for pair in range(0, groups // SUB, 2):
-        blocks = (pair, pair + 1)
-        ratio = [core_half(shrink, block, groups, True) for block in blocks]
-        factor = [core_half(weight, block, groups, True) for block in blocks]
-
-        def step(token, states):
-            result = []
-            for which, block in enumerate(blocks):
-                at = token_row(block, token, tokens)
-                row = grad_filtered[at, :]
-                now = [r * s + row for r, s in zip(ratio[which], states[which])]
-                partial[at, :] = tree_sum([w * s for w, s in zip(factor[which], now)])
-                result.append(now)
-            return result
-
-        over_tokens(0, tokens, step, [half_of(after.at[0], block, groups) for block in blocks], backward=True)
-
-
-def grad_rows(tokens, groups, grad_filtered, shrink, weight, after_mine, after_other, partial, key, value, normed, grad_query,
+def grad_mine(tokens, groups, grad_filtered, local_adjoints, shrink, weight, after, partial):
+    steps = tokens // STEP
+    for block in range(groups // SUB):
+        rising, passed = powers(core_half(shrink, block, groups, True), core_half(weight, block, groups, True))
+        tap = taps(shrink, weight, block, groups)
+
+        def advance(step, entering):
+            states = [s + e for s, e in zip(boundary(local_adjoints, block, step, steps, True), entering)]
+            rows = [grad_filtered[token_row(block, step * STEP + inner, tokens), :] for inner in range(STEP)]
+            for inner in range(STEP):
+                own = [tap[on - inner] * rows[on] for on in range(inner, STEP)]
+                partial[token_row(block, step * STEP + inner, tokens), :] = tree_sum(
+                    [w * s for w, s in zip(rising[STEP - 1 - inner], states)] + own
+                )
+            return [p * e for p, e in zip(passed, entering)]
+
+        over_steps(0, steps, 4, advance, half_of(after.at[0], block, groups), backward=True)
+
+
+def grad_rows(tokens, groups, local_adjoints, shrink, weight, after_mine, after_other, partial, key, value, normed, grad_query,
               grad_key, grad_value, grad_residue, normed_out, grad_query_out,
-              total, dense, key_out, value_out, residue_out, sent, whole_sent):
+              total, dense, factors, key_out, value_out, residue_out, sent, whole_sent):
     half = HALF_MODES * groups
     core = lax.axis_index("core")
     total[my_rows(half), :] = after_mine[1]
@@ -410,20 +469,28 @@
 
     pairs = ((key_out, grad_key), (value_out, grad_value))
 
+    for block in range(blocks):
+        rising, passed = powers(core_half(shrink, block, groups, False), core_half(weight, block, groups, False))
+        for power, values in enumerate(rising + [passed]):
+            for mode in range(HALF_MODES):
+                factors[block, power, mode] = values[mode]
+
     def chunk(turn, states):
         tile = tiles - 1 - turn
         first = pl.multiple_of(tile * ROWS16, ROWS16)
         rows = pl.ds(first, ROWS16)
         states = [list(part) for part in states]
         for block in range(blocks):
-            ratio = core_half(shrink, block, groups, False)
-            factor = core_half(weight, block, groups, False)
-            for inner in range(ROWS16 - 1, -1, -1):
-                at = token_row(block, first + inner, tokens)
-                row = grad_filtered[at, :]
-                states[block] = [r * s + row for r, s in zip(ratio, states[block])]
-                part = partial[at, :] + tree_sum([w * s for w, s in zip(factor, states[block])])
-                dense[block, inner * SUB : (inner + 1) * SUB, :] = part
+            *rising, passed = [[factors[block, power, mode] for mode in range(HALF_MODES)] for power in range(STEP + 1)]
+            for step in range(ROWS16 // STEP - 1, -1, -1):
+                local = boundary(local_adjoints, block, tile * (ROWS16 // STEP) + step, tokens // STEP, False)
+                behind = [s + e for s, e in zip(local, states[block])]
+                for inner in range(STEP):
+                    token = step * STEP + inner
+                    part = tree_sum([w * s for w, s in zip(rising[STEP - 1 - inner], behind)])
+                    part = part + partial[token_row(block, first + token, tokens), :]
+                    dense[block, token * SUB : (token + 1) * SUB, :] = part
+                states[block] = [p * e for p, e in zip(passed, states[block])]
             for group in range(block * SUB, (block + 1) * SUB):
                 part = dense[block, pl.ds(group % SUB, ROWS16, stride=SUB), :]
                 key_out[rows, lanes_of(group)] = (part * tile_of(value, first, group)).astype(bf16)
@@ -455,6 +522,7 @@
     dense = shaped(tokens * groups + SUB, LANES)
     modal = shaped(2 * half + groups, LANES)
     halved = shaped(half, LANES)
+    boundaries = shaped(tokens // STEP * 2 * half, LANES)
     two_halves = shaped(2, half, LANES)
     square = shaped(tokens, LANES)
     modal_scratch = pltpu.VMEM((2 * half + groups, LANES), f32)
@@ -463,9 +531,9 @@
     bind = functools.partial
 
     inputs = (key_rows, value_rows, decay_rate, residue, norm_gain[None, :])
-    product, keep, send, shrink, whole, key_near, value_near, rate_near, residue_near, gain = call(
+    product, local_states, keep, send, shrink, whole, key_near, value_near, rate_near, residue_near, gain = call(
         bind(local_ends, tokens, groups),
-        (dense, halved, halved, modal, halved, natural, natural, rates, rates, shaped(1, channels)),
+        (dense, boundaries, halved, halved, modal, halved, natural, natural, rates, rates, shaped(1, channels)),
         *[pltpu.with_memory_space_constraint(array, pltpu.HBM) for array in inputs],
         in_specs=[in_hbm] * len(inputs),
         scratch=[modal_scratch, pltpu.SemaphoreType.DMA((2 * len(CHUNKS) + 3,))],
@@ -483,19 +551,21 @@
     entry_mine, entry_send = call(core_states, (halved, halved), whole, chip_state, keep, recv)
     entry_other = swap(entry_send, "core")
 
-    partial = call(bind(filter_mine, tokens, groups), dense, product, shrink, weight, entry_mine)
+    partial = call(bind(filter_mine, tokens, groups), dense, product, local_states, shrink, weight, entry_mine)
     filtered, curved, sums = call(
         bind(filter_other, tokens, groups),
         (dense, dense, shaped(2, tokens)),
-        product, shrink, weight, entry_other, partial, asked, squared,
+        local_states, shrink, weight, entry_other, partial, asked, squared,
         scratch=[token_scratch, token_scratch],
     )
     other_sums = swap(sums, "tp")
-
-    inverse, slope, grad_filtered, keep, send = call(
+    product, sums = lax.optimization_barrier((product, sums))
+    product_sums = call(bind(step_sums, tokens, groups), boundaries, product, shrink)
+
+    inverse, slope, grad_filtered, local_adjoints, keep, send = call(
         bind(local_adjoint, tokens, groups),
-        (square, square, dense, two_halves, two_halves),
-        sums, other_sums, asked, curved, product, shrink, scale_dense, entry_mine, entry_other,
+        (square, square, dense, boundaries, two_halves, two_halves),
+        sums, other_sums, asked, curved, product, product_sums, shrink, scale_dense, entry_mine, entry_other,
     )
     recv = swap(send, "core")
     normed_near, grad_query_near = call(
@@ -511,14 +581,15 @@
     )
     after_other = swap(after_send, "core")
 
-    partial = call(bind(grad_mine, tokens, groups), dense, grad_filtered, shrink, weight, after_mine)
+    partial = call(bind(grad_mine, tokens, groups), dense, grad_filtered, local_adjoints, shrink, weight, after_mine)
     grad_key, grad_value, grad_residue, normed_out, grad_query = call(
         bind(grad_rows, tokens, groups),
         (natural, natural, rates, natural, natural),
-        grad_filtered, shrink, weight, after_mine, after_other, partial, key_near, value_near, normed_near, grad_query_near,
+        local_adjoints, shrink, weight, after_mine, after_other, partial, key_near, value_near, normed_near, grad_query_near,
         out_specs=(in_hbm,) * 5,
         scratch=[
-            modal_scratch, pltpu.VMEM((groups // SUB, ROWS16 * SUB + SUB, LANES), f32), natural_scratch, natural_scratch,
+            modal_scratch, pltpu.VMEM((groups // SUB, ROWS16 * SUB + SUB, LANES), f32),
+            pltpu.VMEM((groups // SUB, STEP + 1, HALF_MODES, SUB, LANES), f32), natural_scratch, natural_scratch,
             pltpu.VMEM((MODES, channels), f32), pltpu.SemaphoreType.DMA((2, tokens // ROWS16)), pltpu.SemaphoreType.DMA((3,)),
         ],
     )

time: 92.8 us -> 91.7 us (0.988)
  waiting for transfers between devices: 1.33 us -> 0.2 us
    ppermute x5, waiting for transfers between devices: 1.33 us -> 0.2 us  [swap(): return lax.ppermute(value, axis, [(0, 1), (1, 0)])]
    pallas_call x14 -> x15, Pallas kernels: 15.5 us -> 15.5 us  [call(): pl.pallas_call(body, out_shape=out_shape, in_specs=in_specs or [in_vmem]...]
  transfers between devices with their start and end apart: 5 -> 5, of which waited for: 1 -> 1; matrix products, arithmetic and copies ran while one was open for 0% -> 0% of each run, Pallas kernels for 5% -> 6%
where the time goes in v4:
time: 91.7 us; the launch traced here: 91.5 us
  blocking collectives  62.1 us (68%)
  Pallas kernels  15.5 us (17%)
  starting transfers between devices  12.9 us (14%)
    all_to_all x1, blocking collectives, on_device(): totals = lax.all_to_all(total.reshape(chips, cut, LANES), CHIP_AXES, 0, 0)  20.2 us
    pallas_call x15, Pallas kernels, call(): pl.pallas_call(body, out_shape=out_shape, in_specs=in_specs or [in_vmem]...  15.5 us
    all_to_all x1, blocking collectives, on_device(): chip_state = lax.all_to_all(before, CHIP_AXES, 0, 0)  14.4 us
    all_to_all x1, blocking collectives, on_device(): totals = lax.all_to_all(total, CHIP_AXES, 0, 0)  14.2 us
    all_to_all x1, blocking collectives, on_device(): chip_state = lax.all_to_all(before, CHIP_AXES, 0, 0).reshape(half, LANES)  13.3 us
    ppermute x5, starting transfers between devices, swap(): return lax.ppermute(value, axis, [(0, 1), (1, 0)])  12.9 us
  transfers between devices with their start and end apart: 5, of which 1 were waited for; matrix products, arithmetic and copies ran while one was open for 0% of the time, Pallas kernels for 6%

profile of v4, /device:TPU:1, one launch (start us, length us, event | category | flops | bytes accessed | tf_op | source)
XLA Modules:
  0.0 91.5 jit_solution(6379829712794738922)
XLA Ops:
  0.6 0.0 copy-start.1
  0.6 0.0 copy-start
  0.7 3.0 %shard_map.110 = (f32[4104,128]{1,0:T(8,128)S(1)}, f32[8192,128]{1,0:T(8,128)S(1)}, f32[128,128]{1,0:T(8,128)S(1)}, f32[128,128]{1,0:T(8,128)S(1)}, f32[288,128]...) custom-call(bf16[128,4096]{1,0:T(8,128)(2,1)} %key.1, ...), custom_call_target="tpu_custom_call" | custom-call | tf_op jit(solution)/shard_map/pallas_call | solution.py:33
  3.7 3.3 %collective-permute-start = (f32[128,128]{1,0:T(8,128)S(1)}, f32[128,128]{1,0:T(8,128)S(1)}, u32[]{:S(2)}, u32[]{:S(2)}) collective-permute-start(f32[128,128]{1,0:T(8,128)S(1)} %get-tuple-element.56), channel_id=1, source_target_pairs={{0,2},{2,0},{1,3},{3,1},{4,6},{6,4},{5,7},{7,5},{8,10},{10,8},{9,1... | collective-permute-start | bytes 196616 | tf_op jit(solution)/shard_map/ppermute | solution.py:511
  7.0 0.0 copy-done.1
  7.0 0.0 copy-done
  7.0 1.0 %shard_map.111 = (f32[4104,128]{1,0:T(8,128)S(1)}, f32[4104,128]{1,0:T(8,128)S(1)}, f32[288,128]{1,0:T(8,128)S(1)}, f32[288,128]{1,0:T(8,128)S(1)}) custom-call(bf16[128,4096]{1,0:T(8,128)(2,1)S(1)} %copy-done, bf16[128,4096]{1,0:T(8,128)(2,1)S(1)} %copy-done.1, f32[1,4096]{1,0:T(1,128)S(1)} %get-tuple-element.50.gain, ...), custom_call_target="tpu_custom_call" | custom-call | tf_op jit(solution)/shard_map/pallas_call | solution.py:33
  8.0 0.0 collective-permute-done.recv
  8.0 20.2 %all_to_all.20.totals = f32[64,2,128]{2,1,0:T(2,128)S(1)} all-to-all(f32[64,2,128]{2,1,0:T(2,128)S(1)} %bitcast.7), channel_id=1, replica_groups=mesh['x'=4,'yl'=2,'z'=8,'core'=2,'tp'=2] {'x','yl','z'}, dimensions={0} | all-to-all | bytes 131072 | tf_op jit(solution)/shard_map/all_to_all | solution.py:548
  28.2 0.1 shard_map.113
  28.4 13.3 %all_to_all.21 = f32[64,2,128]{2,1,0:T(2,128)S(1)} all-to-all(f32[64,2,128]{2,1,0:T(2,128)S(1)} %shard_map.113), channel_id=1, replica_groups=mesh['x'=4,'yl'=2,'z'=8,'core'=2,'tp'=2] {'x','yl','z'}, dimensions={0} | all-to-all | bytes 131072 | tf_op jit(solution)/shard_map/all_to_all | solution.py:550
  41.7 2.9 %collective-permute-start.1 = (f32[128,128]{1,0:T(8,128)S(1)}, f32[128,128]{1,0:T(8,128)S(1)}, u32[]{:S(2)}, u32[]{:S(2)}) collective-permute-start(f32[128,128]{1,0:T(8,128)S(1)} %get-tuple-element.59), channel_id=1, source_target_pairs={{0,2},{2,0},{1,3},{3,1},{4,6},{6,4},{5,7},{7,5},{8,10},{10,8},{9,1... | collective-permute-start | bytes 196616 | tf_op jit(solution)/shard_map/ppermute | solution.py:511
  44.7 1.1 %shard_map.115.partial = f32[4104,128]{1,0:T(8,128)S(1)} custom-call(f32[4104,128]{1,0:T(8,128)S(1)} %get-tuple-element.66.product, f32[8192,128]{1,0:T(8,128)S(1)} %get-tuple-element.48.local_states, f32[288,128]{1,0:T(8,128)S(1)} %get-tuple-element.49.shrink, f32[288,128]{1,0:T(8,128)S(1)} %get-tuple-element.53.weight, ...), custom_call_target="tpu_custom_call" | custom-call | tf_op jit(solution)/shard_map/pallas_call | solution.py:33
  45.8 0.0 collective-permute-done.1.entry.entry_other
  45.8 1.6 %shard_map.116 = (f32[4104,128]{1,0:T(8,128)S(1)}, f32[4104,128]{1,0:T(8,128)S(1)}, f32[2,128]{1,0:T(2,128)S(1)}) custom-call(f32[8192,128]{1,0:T(8,128)S(1)} %get-tuple-element.48.local_states, f32[288,128]{1,0:T(8,128)S(1)} %get-tuple-element.49.shrink, f32[288,128]{1,0:T(8,128)S(1)} %get-tuple-element.53.weight, ...), custom_call_target="tpu_custom_call" | custom-call | tf_op jit(solution)/shard_map/pallas_call | solution.py:33
  47.4 2.7 %collective-permute-start.2 = (f32[2,128]{1,0:T(2,128)S(1)}, f32[2,128]{1,0:T(2,128)S(1)}, u32[]{:S(2)}, u32[]{:S(2)}) collective-permute-start(f32[2,128]{1,0:T(2,128)S(1)} %get-tuple-element.64.sums), channel_id=1, source_target_pairs={{0,1},{1,0},{2,3},{3,2},{4,5},{5,4},{6,7},{7,6},{8,9},{9,8},{10,11... | collective-permute-start | bytes 3080 | tf_op jit(solution)/shard_map/ppermute | solution.py:511
  50.1 1.1 %shard_map.117.product_sums = f32[8192,128]{1,0:T(8,128)S(1)} custom-call(f32[4104,128]{1,0:T(8,128)S(1)} %get-tuple-element.66.product, f32[288,128]{1,0:T(8,128)S(1)} %get-tuple-element.49.shrink), custom_call_target="tpu_custom_call" | custom-call | tf_op jit(solution)/shard_map/pallas_call | solution.py:33
  51.2 0.2 collective-permute-done.2.other_sums
  51.4 2.7 %shard_map.118 = (f32[128,128]{1,0:T(8,128)S(1)}, f32[128,128]{1,0:T(8,128)S(1)}, f32[4104,128]{1,0:T(8,128)S(1)}, f32[8192,128]{1,0:T(8,128)S(1)}, f32[2,128,12...) custom-call(f32[2,128]{1,0:T(2,128)S(1)} %get-tuple-element.64.sums, f32[2,128]{1,0:T(2,128)S(1)} %collective-permute-done.2.other_sums, ...), custom_call_target="tpu_custom_call" | custom-call | tf_op jit(solution)/shard_map/pallas_call | solution.py:33
  54.1 1.3 %collective-permute-start.3 = (f32[2,128,128]{2,1,0:T(8,128)S(1)}, f32[2,128,128]{2,1,0:T(8,128)S(1)}, u32[]{:S(2)}, u32[]{:S(2)}) collective-permute-start(f32[2,128,128]{2,1,0:T(8,128)S(1)} %get-tuple-element.70), channel_id=1, source_target_pairs={{0,2},{2,0},{1,3},{3,1},{4,6},{6,4},{5,7},{7,5},{8,10},{10,8},{9,1... | collective-permute-start | bytes 393224 | tf_op jit(solution)/shard_map/ppermute | solution.py:511
  55.4 1.0 %shard_map.119 = (bf16[128,4096]{1,0:T(8,128)(2,1)S(1)}, bf16[128,4096]{1,0:T(8,128)(2,1)S(1)}) custom-call(f32[128,128]{1,0:T(8,128)S(1)} %get-tuple-element.71.inverse, f32[128,128]{1,0:T(8,128)S(1)} %get-tuple-element.72.slope, f32[4104,128]{1,0:T(8,128)S(1)} %get-tuple-element.73.filtered, bf16[128,4096]{1,0:T(8,128)(2,1)S(1)} %copy-done, ...), custom_call_target="tpu_custom_call" | custom-call | tf_op jit(solution)/shard_map/pallas_call | solution.py:33
  56.3 0.0 collective-permute-done.3.recv
  56.4 0.1 shard_map.120
  56.4 14.2 %all_to_all.22.totals = f32[64,2,2,128]{3,2,1,0:T(2,128)S(1)} all-to-all(f32[64,2,2,128]{3,2,1,0:T(2,128)S(1)} %shard_map.120), channel_id=1, replica_groups=mesh['x'=4,'yl'=2,'z'=8,'core'=2,'tp'=2] {'x','yl','z'}, dimensions={0} | all-to-all | bytes 262144 | tf_op jit(solution)/shard_map/all_to_all | solution.py:576
  70.6 0.2 shard_map.121
  70.8 14.4 %all_to_all.23.chip_state = f32[64,2,2,128]{3,2,1,0:T(2,128)S(1)} all-to-all(f32[64,2,2,128]{3,2,1,0:T(2,128)S(1)} %shard_map.121), channel_id=1, replica_groups=mesh['x'=4,'yl'=2,'z'=8,'core'=2,'tp'=2] {'x','yl','z'}, dimensions={0} | all-to-all | bytes 262144 | tf_op jit(solution)/shard_map/all_to_all | solution.py:578
  85.1 0.1 shard_map.122
  85.2 2.6 %collective-permute-start.4 = (f32[2,128,128]{2,1,0:T(8,128)S(1)}, f32[2,128,128]{2,1,0:T(8,128)S(1)}, u32[]{:S(2)}, u32[]{:S(2)}) collective-permute-start(f32[2,128,128]{2,1,0:T(8,128)S(1)} %get-tuple-element.78), channel_id=1, source_target_pairs={{0,2},{2,0},{1,3},{3,1},{4,6},{6,4},{5,7},{7,5},{8,10},{10,8},{9,1... | collective-permute-start | bytes 393224 | tf_op jit(solution)/shard_map/ppermute | solution.py:511
  87.8 1.2 %shard_map.123.partial = f32[4104,128]{1,0:T(8,128)S(1)} custom-call(f32[4104,128]{1,0:T(8,128)S(1)} %get-tuple-element.79.grad_filtered, f32[8192,128]{1,0:T(8,128)S(1)} %get-tuple-element.68.local_adjoints, f32[288,128]{1,0:T(8,128)S(1)} %get-tuple-element.49.shrink, f32[288,128]{1,0:T(8,128)S(1)} %get-tuple-element.53.weight, ...), custom_call_target="tpu_custom_call" | custom-call | tf_op jit(solution)/shard_map/pallas_call | solution.py:33
  89.0 0.0 collective-permute-done.4.after_other
  89.0 2.4 %shard_map.124 = (bf16[128,4096]{1,0:T(8,128)(2,1)}, bf16[128,4096]{1,0:T(8,128)(2,1)}, f32[8,4096]{1,0:T(8,128)}, bf16[128,4096]{1,0:T(8,128)(2,1)}, bf16[128,4096]{1,0:T(8,128)(2,1)}) custom-call(f32[8192,128]{1,0:T(8,128)S(1)} %get-tuple-element.68.local_adjoints, f32[288,128]{1,0:T(8,128)S(1)} %get-tuple-element.49.shrink, ...), custom_call_target="tpu_custom_call" | custom-call | tf_op jit(solution)/shard_map/pallas_call | solution.py:33
  (2 shorter events, 0.0 us)
Async XLA Ops:
  0.6 6.4 %copy-start.1 = (bf16[128,4096]{1,0:T(8,128)(2,1)S(1)}, bf16[128,4096]{1,0:T(8,128)(2,1)}, u32[]{:S(2)}) copy-start(bf16[128,4096]{1,0:T(8,128)(2,1)} %grad.3) | copy-start | bytes 3145732
  0.6 6.4 %copy-start = (bf16[128,4096]{1,0:T(8,128)(2,1)S(1)}, bf16[128,4096]{1,0:T(8,128)(2,1)}, u32[]{:S(2)}) copy-start(bf16[128,4096]{1,0:T(8,128)(2,1)} %query.3) | copy-start | bytes 3145732
  3.7 4.3 %collective-permute-start = (f32[128,128]{1,0:T(8,128)S(1)}, f32[128,128]{1,0:T(8,128)S(1)}, u32[]{:S(2)}, u32[]{:S(2)}) collective-permute-start(f32[128,128]{1,0:T(8,128)S(1)} %get-tuple-element.56), channel_id=1, source_target_pairs={{0,2},{2,0},{1,3},{3,1},{4,6},{6,4},{5,7},{7,5},{8,10},{10,8},{9,1... | collective-permute-start | bytes 196616 | tf_op jit(solution)/shard_map/ppermute | solution.py:511
  41.7 4.1 %collective-permute-start.1 = (f32[128,128]{1,0:T(8,128)S(1)}, f32[128,128]{1,0:T(8,128)S(1)}, u32[]{:S(2)}, u32[]{:S(2)}) collective-permute-start(f32[128,128]{1,0:T(8,128)S(1)} %get-tuple-element.59), channel_id=1, source_target_pairs={{0,2},{2,0},{1,3},{3,1},{4,6},{6,4},{5,7},{7,5},{8,10},{10,8},{9,1... | collective-permute-start | bytes 196616 | tf_op jit(solution)/shard_map/ppermute | solution.py:511
  47.4 4.0 %collective-permute-start.2 = (f32[2,128]{1,0:T(2,128)S(1)}, f32[2,128]{1,0:T(2,128)S(1)}, u32[]{:S(2)}, u32[]{:S(2)}) collective-permute-start(f32[2,128]{1,0:T(2,128)S(1)} %get-tuple-element.64.sums), channel_id=1, source_target_pairs={{0,1},{1,0},{2,3},{3,2},{4,5},{5,4},{6,7},{7,6},{8,9},{9,8},{10,11... | collective-permute-start | bytes 3080 | tf_op jit(solution)/shard_map/ppermute | solution.py:511
  54.1 2.3 %collective-permute-start.3 = (f32[2,128,128]{2,1,0:T(8,128)S(1)}, f32[2,128,128]{2,1,0:T(8,128)S(1)}, u32[]{:S(2)}, u32[]{:S(2)}) collective-permute-start(f32[2,128,128]{2,1,0:T(8,128)S(1)} %get-tuple-element.70), channel_id=1, source_target_pairs={{0,2},{2,0},{1,3},{3,1},{4,6},{6,4},{5,7},{7,5},{8,10},{10,8},{9,1... | collective-permute-start | bytes 393224 | tf_op jit(solution)/shard_map/ppermute | solution.py:511
  85.2 3.8 %collective-permute-start.4 = (f32[2,128,128]{2,1,0:T(8,128)S(1)}, f32[2,128,128]{2,1,0:T(8,128)S(1)}, u32[]{:S(2)}, u32[]{:S(2)}) collective-permute-start(f32[2,128,128]{2,1,0:T(8,128)S(1)} %get-tuple-element.78), channel_id=1, source_target_pairs={{0,2},{2,0},{1,3},{3,1},{4,6},{6,4},{5,7},{7,5},{8,10},{10,8},{9,1... | collective-permute-start | bytes 393224 | tf_op jit(solution)/shard_map/ppermute | solution.py:511

commit v5 on v4

--- a/solution.py
+++ b/solution.py
@@ -428,8 +428,10 @@
     other[1] = summed
 
 
-def grad_mine(tokens, groups, grad_filtered, local_adjoints, shrink, weight, after, partial):
+def grad_mine(tokens, groups, grad_filtered, local_adjoints, shrink, weight, after, normed, partial, normed_out, sent):
     steps = tokens // STEP
+    copy = pltpu.make_async_copy(normed, normed_out, sent)
+    copy.start()
     for block in range(groups // SUB):
         rising, passed = powers(core_half(shrink, block, groups, True), core_half(weight, block, groups, True))
         tap = taps(shrink, weight, block, groups)
@@ -445,10 +447,11 @@
             return [p * e for p, e in zip(passed, entering)]
 
         over_steps(0, steps, 4, advance, half_of(after.at[0], block, groups), backward=True)
-
-
-def grad_rows(tokens, groups, local_adjoints, shrink, weight, after_mine, after_other, partial, key, value, normed, grad_query,
-              grad_key, grad_value, grad_residue, normed_out, grad_query_out,
+    copy.wait()
+
+
+def grad_rows(tokens, groups, local_adjoints, shrink, weight, after_mine, after_other, partial, key, value, grad_query,
+              grad_key, grad_value, grad_residue, grad_query_out,
               total, dense, factors, key_out, value_out, residue_out, sent, whole_sent):
     half = HALF_MODES * groups
     core = lax.axis_index("core")
@@ -459,7 +462,7 @@
     whole_copies = [
         pltpu.make_async_copy(source, target, whole_sent.at[which])
         for which, (source, target) in enumerate(
-            ((normed, normed_out), (grad_query, grad_query_out), (residue_out, grad_residue))
+            ((grad_query, grad_query_out), (residue_out, grad_residue))
         )
     ]
     for copy in whole_copies:
@@ -581,16 +584,22 @@
     )
     after_other = swap(after_send, "core")
 
-    partial = call(bind(grad_mine, tokens, groups), dense, grad_filtered, local_adjoints, shrink, weight, after_mine)
-    grad_key, grad_value, grad_residue, normed_out, grad_query = call(
+    partial, normed_out = call(
+        bind(grad_mine, tokens, groups),
+        (dense, natural),
+        grad_filtered, local_adjoints, shrink, weight, after_mine, normed_near,
+        out_specs=(in_vmem, in_hbm),
+        scratch=[pltpu.SemaphoreType.DMA],
+    )
+    grad_key, grad_value, grad_residue, grad_query = call(
         bind(grad_rows, tokens, groups),
-        (natural, natural, rates, natural, natural),
-        local_adjoints, shrink, weight, after_mine, after_other, partial, key_near, value_near, normed_near, grad_query_near,
-        out_specs=(in_hbm,) * 5,
+        (natural, natural, rates, natural),
+        local_adjoints, shrink, weight, after_mine, after_other, partial, key_near, value_near, grad_query_near,
+        out_specs=(in_hbm,) * 4,
         scratch=[
             modal_scratch, pltpu.VMEM((groups // SUB, ROWS16 * SUB + SUB, LANES), f32),
             pltpu.VMEM((groups // SUB, STEP + 1, HALF_MODES, SUB, LANES), f32), natural_scratch, natural_scratch,
-            pltpu.VMEM((MODES, channels), f32), pltpu.SemaphoreType.DMA((2, tokens // ROWS16)), pltpu.SemaphoreType.DMA((3,)),
+            pltpu.VMEM((MODES, channels), f32), pltpu.SemaphoreType.DMA((2, tokens // ROWS16)), pltpu.SemaphoreType.DMA((2,)),
         ],
     )
     return (normed_out, grad_query, grad_key, grad_value, grad_residue)

time: 91.7 us -> 91.7 us (level)
  no operation moved by 1% of the time
where the time goes in v5:
time: 91.7 us; the launch traced here: 91.5 us
  blocking collectives  62.1 us (68%)
  Pallas kernels  15.5 us (17%)
  starting transfers between devices  12.9 us (14%)
    all_to_all x1, blocking collectives, on_device(): totals = lax.all_to_all(total.reshape(chips, cut, LANES), CHIP_AXES, 0, 0)  20.2 us
    pallas_call x15, Pallas kernels, call(): pl.pallas_call(body, out_shape=out_shape, in_specs=in_specs or [in_vmem]...  15.5 us
    all_to_all x1, blocking collectives, on_device(): chip_state = lax.all_to_all(before, CHIP_AXES, 0, 0)  14.4 us
    all_to_all x1, blocking collectives, on_device(): totals = lax.all_to_all(total, CHIP_AXES, 0, 0)  14.2 us
    all_to_all x1, blocking collectives, on_device(): chip_state = lax.all_to_all(before, CHIP_AXES, 0, 0).reshape(half, LANES)  13.3 us
    ppermute x5, starting transfers between devices, swap(): return lax.ppermute(value, axis, [(0, 1), (1, 0)])  12.9 us
  transfers between devices with their start and end apart: 5, of which 1 were waited for; matrix products, arithmetic and copies ran while one was open for 0% of the time, Pallas kernels for 6%

profile of v5, /device:TPU:1, one launch (start us, length us, event | category | flops | bytes accessed | tf_op | source)
XLA Modules:
  0.0 91.5 jit_solution(11651462212688621841)
XLA Ops:
  0.6 0.0 copy-start.1
  0.6 0.0 copy-start
  0.7 3.0 %shard_map.110 = (f32[4104,128]{1,0:T(8,128)S(1)}, f32[8192,128]{1,0:T(8,128)S(1)}, f32[128,128]{1,0:T(8,128)S(1)}, f32[128,128]{1,0:T(8,128)S(1)}, f32[288,128]...) custom-call(bf16[128,4096]{1,0:T(8,128)(2,1)} %key.1, ...), custom_call_target="tpu_custom_call" | custom-call | tf_op jit(solution)/shard_map/pallas_call | solution.py:33
  3.7 3.3 %collective-permute-start = (f32[128,128]{1,0:T(8,128)S(1)}, f32[128,128]{1,0:T(8,128)S(1)}, u32[]{:S(2)}, u32[]{:S(2)}) collective-permute-start(f32[128,128]{1,0:T(8,128)S(1)} %get-tuple-element.57), channel_id=1, source_target_pairs={{0,2},{2,0},{1,3},{3,1},{4,6},{6,4},{5,7},{7,5},{8,10},{10,8},{9,1... | collective-permute-start | bytes 196616 | tf_op jit(solution)/shard_map/ppermute | solution.py:514
  7.0 0.0 copy-done.1
  7.0 0.0 copy-done
  7.0 1.0 %shard_map.111 = (f32[4104,128]{1,0:T(8,128)S(1)}, f32[4104,128]{1,0:T(8,128)S(1)}, f32[288,128]{1,0:T(8,128)S(1)}, f32[288,128]{1,0:T(8,128)S(1)}) custom-call(bf16[128,4096]{1,0:T(8,128)(2,1)S(1)} %copy-done, bf16[128,4096]{1,0:T(8,128)(2,1)S(1)} %copy-done.1, f32[1,4096]{1,0:T(1,128)S(1)} %get-tuple-element.51.gain, ...), custom_call_target="tpu_custom_call" | custom-call | tf_op jit(solution)/shard_map/pallas_call | solution.py:33
  8.0 0.0 collective-permute-done.recv
  8.0 20.2 %all_to_all.20.totals = f32[64,2,128]{2,1,0:T(2,128)S(1)} all-to-all(f32[64,2,128]{2,1,0:T(2,128)S(1)} %bitcast.7), channel_id=1, replica_groups=mesh['x'=4,'yl'=2,'z'=8,'core'=2,'tp'=2] {'x','yl','z'}, dimensions={0} | all-to-all | bytes 131072 | tf_op jit(solution)/shard_map/all_to_all | solution.py:551
  28.2 0.1 shard_map.113
  28.4 13.3 %all_to_all.21 = f32[64,2,128]{2,1,0:T(2,128)S(1)} all-to-all(f32[64,2,128]{2,1,0:T(2,128)S(1)} %shard_map.113), channel_id=1, replica_groups=mesh['x'=4,'yl'=2,'z'=8,'core'=2,'tp'=2] {'x','yl','z'}, dimensions={0} | all-to-all | bytes 131072 | tf_op jit(solution)/shard_map/all_to_all | solution.py:553
  41.7 2.9 %collective-permute-start.1 = (f32[128,128]{1,0:T(8,128)S(1)}, f32[128,128]{1,0:T(8,128)S(1)}, u32[]{:S(2)}, u32[]{:S(2)}) collective-permute-start(f32[128,128]{1,0:T(8,128)S(1)} %get-tuple-element.60), channel_id=1, source_target_pairs={{0,2},{2,0},{1,3},{3,1},{4,6},{6,4},{5,7},{7,5},{8,10},{10,8},{9,1... | collective-permute-start | bytes 196616 | tf_op jit(solution)/shard_map/ppermute | solution.py:514
  44.6 1.1 %shard_map.115.partial = f32[4104,128]{1,0:T(8,128)S(1)} custom-call(f32[4104,128]{1,0:T(8,128)S(1)} %get-tuple-element.67.product, f32[8192,128]{1,0:T(8,128)S(1)} %get-tuple-element.49.local_states, f32[288,128]{1,0:T(8,128)S(1)} %get-tuple-element.50.shrink, f32[288,128]{1,0:T(8,128)S(1)} %get-tuple-element.54.weight, ...), custom_call_target="tpu_custom_call" | custom-call | tf_op jit(solution)/shard_map/pallas_call | solution.py:33
  45.8 0.0 collective-permute-done.1.entry.entry_other
  45.8 1.6 %shard_map.116 = (f32[4104,128]{1,0:T(8,128)S(1)}, f32[4104,128]{1,0:T(8,128)S(1)}, f32[2,128]{1,0:T(2,128)S(1)}) custom-call(f32[8192,128]{1,0:T(8,128)S(1)} %get-tuple-element.49.local_states, f32[288,128]{1,0:T(8,128)S(1)} %get-tuple-element.50.shrink, f32[288,128]{1,0:T(8,128)S(1)} %get-tuple-element.54.weight, ...), custom_call_target="tpu_custom_call" | custom-call | tf_op jit(solution)/shard_map/pallas_call | solution.py:33
  47.4 2.7 %collective-permute-start.2 = (f32[2,128]{1,0:T(2,128)S(1)}, f32[2,128]{1,0:T(2,128)S(1)}, u32[]{:S(2)}, u32[]{:S(2)}) collective-permute-start(f32[2,128]{1,0:T(2,128)S(1)} %get-tuple-element.65.sums), channel_id=1, source_target_pairs={{0,1},{1,0},{2,3},{3,2},{4,5},{5,4},{6,7},{7,6},{8,9},{9,8},{10,11... | collective-permute-start | bytes 3080 | tf_op jit(solution)/shard_map/ppermute | solution.py:514
  50.1 1.1 %shard_map.117.product_sums = f32[8192,128]{1,0:T(8,128)S(1)} custom-call(f32[4104,128]{1,0:T(8,128)S(1)} %get-tuple-element.67.product, f32[288,128]{1,0:T(8,128)S(1)} %get-tuple-element.50.shrink), custom_call_target="tpu_custom_call" | custom-call | tf_op jit(solution)/shard_map/pallas_call | solution.py:33
  51.2 0.2 collective-permute-done.2.other_sums
  51.4 2.7 %shard_map.118 = (f32[128,128]{1,0:T(8,128)S(1)}, f32[128,128]{1,0:T(8,128)S(1)}, f32[4104,128]{1,0:T(8,128)S(1)}, f32[8192,128]{1,0:T(8,128)S(1)}, f32[2,128,12...) custom-call(f32[2,128]{1,0:T(2,128)S(1)} %get-tuple-element.65.sums, f32[2,128]{1,0:T(2,128)S(1)} %collective-permute-done.2.other_sums, ...), custom_call_target="tpu_custom_call" | custom-call | tf_op jit(solution)/shard_map/pallas_call | solution.py:33
  54.1 1.3 %collective-permute-start.3 = (f32[2,128,128]{2,1,0:T(8,128)S(1)}, f32[2,128,128]{2,1,0:T(8,128)S(1)}, u32[]{:S(2)}, u32[]{:S(2)}) collective-permute-start(f32[2,128,128]{2,1,0:T(8,128)S(1)} %get-tuple-element.72), channel_id=1, source_target_pairs={{0,2},{2,0},{1,3},{3,1},{4,6},{6,4},{5,7},{7,5},{8,10},{10,8},{9,1... | collective-permute-start | bytes 393224 | tf_op jit(solution)/shard_map/ppermute | solution.py:514
  55.4 1.0 %shard_map.119 = (bf16[128,4096]{1,0:T(8,128)(2,1)S(1)}, bf16[128,4096]{1,0:T(8,128)(2,1)S(1)}) custom-call(f32[128,128]{1,0:T(8,128)S(1)} %get-tuple-element.73.inverse, f32[128,128]{1,0:T(8,128)S(1)} %get-tuple-element.74.slope, f32[4104,128]{1,0:T(8,128)S(1)} %get-tuple-element.75.filtered, bf16[128,4096]{1,0:T(8,128)(2,1)S(1)} %copy-done, ...), custom_call_target="tpu_custom_call" | custom-call | tf_op jit(solution)/shard_map/pallas_call | solution.py:33
  56.3 0.0 collective-permute-done.3.recv
  56.4 0.1 shard_map.120
  56.4 14.2 %all_to_all.22.totals = f32[64,2,2,128]{3,2,1,0:T(2,128)S(1)} all-to-all(f32[64,2,2,128]{3,2,1,0:T(2,128)S(1)} %shard_map.120), channel_id=1, replica_groups=mesh['x'=4,'yl'=2,'z'=8,'core'=2,'tp'=2] {'x','yl','z'}, dimensions={0} | all-to-all | bytes 262144 | tf_op jit(solution)/shard_map/all_to_all | solution.py:579
  70.6 0.2 shard_map.121
  70.8 14.4 %all_to_all.23.chip_state = f32[64,2,2,128]{3,2,1,0:T(2,128)S(1)} all-to-all(f32[64,2,2,128]{3,2,1,0:T(2,128)S(1)} %shard_map.121), channel_id=1, replica_groups=mesh['x'=4,'yl'=2,'z'=8,'core'=2,'tp'=2] {'x','yl','z'}, dimensions={0} | all-to-all | bytes 262144 | tf_op jit(solution)/shard_map/all_to_all | solution.py:581
  85.1 0.1 shard_map.122
  85.2 2.6 %collective-permute-start.4 = (f32[2,128,128]{2,1,0:T(8,128)S(1)}, f32[2,128,128]{2,1,0:T(8,128)S(1)}, u32[]{:S(2)}, u32[]{:S(2)}) collective-permute-start(f32[2,128,128]{2,1,0:T(8,128)S(1)} %get-tuple-element.82), channel_id=1, source_target_pairs={{0,2},{2,0},{1,3},{3,1},{4,6},{6,4},{5,7},{7,5},{8,10},{10,8},{9,1... | collective-permute-start | bytes 393224 | tf_op jit(solution)/shard_map/ppermute | solution.py:514
  87.8 1.2 %shard_map.123 = (f32[4104,128]{1,0:T(8,128)S(1)}, bf16[128,4096]{1,0:T(8,128)(2,1)}) custom-call(f32[4104,128]{1,0:T(8,128)S(1)} %get-tuple-element.69.grad_filtered, f32[8192,128]{1,0:T(8,128)S(1)} %get-tuple-element.70.local_adjoints, f32[288,128]{1,0:T(8,128)S(1)} %get-tuple-element.50.shrink, f32[288,128]{1,0:T(8,128)S(1)} %get-tuple-element.54.weight, ...), custom_call_target="tpu_custom_call" | custom-call | tf_op jit(solution)/shard_map/pallas_call | solution.py:33
  89.0 0.0 collective-permute-done.4.after_other
  89.1 2.4 %shard_map.124 = (bf16[128,4096]{1,0:T(8,128)(2,1)}, bf16[128,4096]{1,0:T(8,128)(2,1)}, f32[8,4096]{1,0:T(8,128)}, bf16[128,4096]{1,0:T(8,128)(2,1)}) custom-call(f32[8192,128]{1,0:T(8,128)S(1)} %get-tuple-element.70.local_adjoints, f32[288,128]{1,0:T(8,128)S(1)} %get-tuple-element.50.shrink, f32[288,128]{1,0:T(8,128)S(1)} %get-tuple-element.54.weight, ...), custom_call_target="tpu_custom_call" | custom-call | tf_op jit(solution)/shard_map/pallas_call | solution.py:33
  (2 shorter events, 0.0 us)
Async XLA Ops:
  0.6 6.4 %copy-start.1 = (bf16[128,4096]{1,0:T(8,128)(2,1)S(1)}, bf16[128,4096]{1,0:T(8,128)(2,1)}, u32[]{:S(2)}) copy-start(bf16[128,4096]{1,0:T(8,128)(2,1)} %grad.3) | copy-start | bytes 3145732
  0.6 6.4 %copy-start = (bf16[128,4096]{1,0:T(8,128)(2,1)S(1)}, bf16[128,4096]{1,0:T(8,128)(2,1)}, u32[]{:S(2)}) copy-start(bf16[128,4096]{1,0:T(8,128)(2,1)} %query.3) | copy-start | bytes 3145732
  3.7 4.3 %collective-permute-start = (f32[128,128]{1,0:T(8,128)S(1)}, f32[128,128]{1,0:T(8,128)S(1)}, u32[]{:S(2)}, u32[]{:S(2)}) collective-permute-start(f32[128,128]{1,0:T(8,128)S(1)} %get-tuple-element.57), channel_id=1, source_target_pairs={{0,2},{2,0},{1,3},{3,1},{4,6},{6,4},{5,7},{7,5},{8,10},{10,8},{9,1... | collective-permute-start | bytes 196616 | tf_op jit(solution)/shard_map/ppermute | solution.py:514
  41.7 4.1 %collective-permute-start.1 = (f32[128,128]{1,0:T(8,128)S(1)}, f32[128,128]{1,0:T(8,128)S(1)}, u32[]{:S(2)}, u32[]{:S(2)}) collective-permute-start(f32[128,128]{1,0:T(8,128)S(1)} %get-tuple-element.60), channel_id=1, source_target_pairs={{0,2},{2,0},{1,3},{3,1},{4,6},{6,4},{5,7},{7,5},{8,10},{10,8},{9,1... | collective-permute-start | bytes 196616 | tf_op jit(solution)/shard_map/ppermute | solution.py:514
  47.4 4.0 %collective-permute-start.2 = (f32[2,128]{1,0:T(2,128)S(1)}, f32[2,128]{1,0:T(2,128)S(1)}, u32[]{:S(2)}, u32[]{:S(2)}) collective-permute-start(f32[2,128]{1,0:T(2,128)S(1)} %get-tuple-element.65.sums), channel_id=1, source_target_pairs={{0,1},{1,0},{2,3},{3,2},{4,5},{5,4},{6,7},{7,6},{8,9},{9,8},{10,11... | collective-permute-start | bytes 3080 | tf_op jit(solution)/shard_map/ppermute | solution.py:514
  54.1 2.3 %collective-permute-start.3 = (f32[2,128,128]{2,1,0:T(8,128)S(1)}, f32[2,128,128]{2,1,0:T(8,128)S(1)}, u32[]{:S(2)}, u32[]{:S(2)}) collective-permute-start(f32[2,128,128]{2,1,0:T(8,128)S(1)} %get-tuple-element.72), channel_id=1, source_target_pairs={{0,2},{2,0},{1,3},{3,1},{4,6},{6,4},{5,7},{7,5},{8,10},{10,8},{9,1... | collective-permute-start | bytes 393224 | tf_op jit(solution)/shard_map/ppermute | solution.py:514
  85.2 3.9 %collective-permute-start.4 = (f32[2,128,128]{2,1,0:T(8,128)S(1)}, f32[2,128,128]{2,1,0:T(8,128)S(1)}, u32[]{:S(2)}, u32[]{:S(2)}) collective-permute-start(f32[2,128,128]{2,1,0:T(8,128)S(1)} %get-tuple-element.82), channel_id=1, source_target_pairs={{0,2},{2,0},{1,3},{3,1},{4,6},{6,4},{5,7},{7,5},{8,10},{10,8},{9,1... | collective-permute-start | bytes 393224 | tf_op jit(solution)/shard_map/ppermute | solution.py:514

commit v6 on v5

--- a/solution.py
+++ b/solution.py
@@ -453,20 +453,6 @@
 def grad_rows(tokens, groups, local_adjoints, shrink, weight, after_mine, after_other, partial, key, value, grad_query,
               grad_key, grad_value, grad_residue, grad_query_out,
               total, dense, factors, key_out, value_out, residue_out, sent, whole_sent):
-    half = HALF_MODES * groups
-    core = lax.axis_index("core")
-    total[my_rows(half), :] = after_mine[1]
-    total[pl.ds(pl.multiple_of((1 - core) * half, half), half), :] = after_other[1]
-    for group in range(groups):
-        residue_out[:, lanes_of(group)] = total[pl.ds(group, MODES, stride=groups), :]
-    whole_copies = [
-        pltpu.make_async_copy(source, target, whole_sent.at[which])
-        for which, (source, target) in enumerate(
-            ((grad_query, grad_query_out), (residue_out, grad_residue))
-        )
-    ]
-    for copy in whole_copies:
-        copy.start()
     blocks = groups // SUB
     tiles = tokens // ROWS16
 
@@ -503,6 +489,20 @@
         return states
 
     lax.fori_loop(0, tiles, chunk, [half_of(after_other.at[0], block, groups) for block in range(blocks)])
+    half = HALF_MODES * groups
+    core = lax.axis_index("core")
+    total[my_rows(half), :] = after_mine[1]
+    total[pl.ds(pl.multiple_of((1 - core) * half, half), half), :] = after_other[1]
+    for group in range(groups):
+        residue_out[:, lanes_of(group)] = total[pl.ds(group, MODES, stride=groups), :]
+    whole_copies = [
+        pltpu.make_async_copy(source, target, whole_sent.at[which])
+        for which, (source, target) in enumerate(
+            ((grad_query, grad_query_out), (residue_out, grad_residue))
+        )
+    ]
+    for copy in whole_copies:
+        copy.start()
     for tile in range(tiles):
         for copy in tile_copies(tile, sent, *pairs):
             copy.wait()

time: 91.7 us -> 92 us (level)
  no operation moved by 1% of the time
where the time goes in v6:
time: 92 us; the launch traced here: 91.7 us
  blocking collectives  62.1 us (68%)
  Pallas kernels  15.8 us (17%)
  starting transfers between devices  12.9 us (14%)
    all_to_all x1, blocking collectives, on_device(): totals = lax.all_to_all(total.reshape(chips, cut, LANES), CHIP_AXES, 0, 0)  20.2 us
    pallas_call x15, Pallas kernels, call(): pl.pallas_call(body, out_shape=out_shape, in_specs=in_specs or [in_vmem]...  15.8 us
    all_to_all x1, blocking collectives, on_device(): chip_state = lax.all_to_all(before, CHIP_AXES, 0, 0)  14.4 us
    all_to_all x1, blocking collectives, on_device(): totals = lax.all_to_all(total, CHIP_AXES, 0, 0)  14.2 us
    all_to_all x1, blocking collectives, on_device(): chip_state = lax.all_to_all(before, CHIP_AXES, 0, 0).reshape(half, LANES)  13.3 us
    ppermute x5, starting transfers between devices, swap(): return lax.ppermute(value, axis, [(0, 1), (1, 0)])  12.9 us
  transfers between devices with their start and end apart: 5, of which 1 were waited for; matrix products, arithmetic and copies ran while one was open for 0% of the time, Pallas kernels for 6%

profile of v6, /device:TPU:1, one launch (start us, length us, event | category | flops | bytes accessed | tf_op | source)
XLA Modules:
  0.0 91.7 jit_solution(14734587629158325440)
XLA Ops:
  0.6 0.0 copy-start.1
  0.6 0.0 copy-start
  0.7 3.0 %shard_map.110 = (f32[4104,128]{1,0:T(8,128)S(1)}, f32[8192,128]{1,0:T(8,128)S(1)}, f32[128,128]{1,0:T(8,128)S(1)}, f32[128,128]{1,0:T(8,128)S(1)}, f32[288,128]...) custom-call(bf16[128,4096]{1,0:T(8,128)(2,1)} %key.1, ...), custom_call_target="tpu_custom_call" | custom-call | tf_op jit(solution)/shard_map/pallas_call | solution.py:33
  3.7 3.3 %collective-permute-start = (f32[128,128]{1,0:T(8,128)S(1)}, f32[128,128]{1,0:T(8,128)S(1)}, u32[]{:S(2)}, u32[]{:S(2)}) collective-permute-start(f32[128,128]{1,0:T(8,128)S(1)} %get-tuple-element.57), channel_id=1, source_target_pairs={{0,2},{2,0},{1,3},{3,1},{4,6},{6,4},{5,7},{7,5},{8,10},{10,8},{9,1... | collective-permute-start | bytes 196616 | tf_op jit(solution)/shard_map/ppermute | solution.py:514
  7.0 0.0 copy-done.1
  7.0 0.0 copy-done
  7.0 1.0 %shard_map.111 = (f32[4104,128]{1,0:T(8,128)S(1)}, f32[4104,128]{1,0:T(8,128)S(1)}, f32[288,128]{1,0:T(8,128)S(1)}, f32[288,128]{1,0:T(8,128)S(1)}) custom-call(bf16[128,4096]{1,0:T(8,128)(2,1)S(1)} %copy-done, bf16[128,4096]{1,0:T(8,128)(2,1)S(1)} %copy-done.1, f32[1,4096]{1,0:T(1,128)S(1)} %get-tuple-element.51.gain, ...), custom_call_target="tpu_custom_call" | custom-call | tf_op jit(solution)/shard_map/pallas_call | solution.py:33
  8.0 0.0 collective-permute-done.recv
  8.0 20.2 %all_to_all.20.totals = f32[64,2,128]{2,1,0:T(2,128)S(1)} all-to-all(f32[64,2,128]{2,1,0:T(2,128)S(1)} %bitcast.7), channel_id=1, replica_groups=mesh['x'=4,'yl'=2,'z'=8,'core'=2,'tp'=2] {'x','yl','z'}, dimensions={0} | all-to-all | bytes 131072 | tf_op jit(solution)/shard_map/all_to_all | solution.py:551
  28.2 0.1 shard_map.113
  28.4 13.3 %all_to_all.21 = f32[64,2,128]{2,1,0:T(2,128)S(1)} all-to-all(f32[64,2,128]{2,1,0:T(2,128)S(1)} %shard_map.113), channel_id=1, replica_groups=mesh['x'=4,'yl'=2,'z'=8,'core'=2,'tp'=2] {'x','yl','z'}, dimensions={0} | all-to-all | bytes 131072 | tf_op jit(solution)/shard_map/all_to_all | solution.py:553
  41.7 2.9 %collective-permute-start.1 = (f32[128,128]{1,0:T(8,128)S(1)}, f32[128,128]{1,0:T(8,128)S(1)}, u32[]{:S(2)}, u32[]{:S(2)}) collective-permute-start(f32[128,128]{1,0:T(8,128)S(1)} %get-tuple-element.60), channel_id=1, source_target_pairs={{0,2},{2,0},{1,3},{3,1},{4,6},{6,4},{5,7},{7,5},{8,10},{10,8},{9,1... | collective-permute-start | bytes 196616 | tf_op jit(solution)/shard_map/ppermute | solution.py:514
  44.6 1.1 %shard_map.115.partial = f32[4104,128]{1,0:T(8,128)S(1)} custom-call(f32[4104,128]{1,0:T(8,128)S(1)} %get-tuple-element.67.product, f32[8192,128]{1,0:T(8,128)S(1)} %get-tuple-element.49.local_states, f32[288,128]{1,0:T(8,128)S(1)} %get-tuple-element.50.shrink, f32[288,128]{1,0:T(8,128)S(1)} %get-tuple-element.54.weight, ...), custom_call_target="tpu_custom_call" | custom-call | tf_op jit(solution)/shard_map/pallas_call | solution.py:33
  45.8 0.0 collective-permute-done.1.entry.entry_other
  45.8 1.6 %shard_map.116 = (f32[4104,128]{1,0:T(8,128)S(1)}, f32[4104,128]{1,0:T(8,128)S(1)}, f32[2,128]{1,0:T(2,128)S(1)}) custom-call(f32[8192,128]{1,0:T(8,128)S(1)} %get-tuple-element.49.local_states, f32[288,128]{1,0:T(8,128)S(1)} %get-tuple-element.50.shrink, f32[288,128]{1,0:T(8,128)S(1)} %get-tuple-element.54.weight, ...), custom_call_target="tpu_custom_call" | custom-call | tf_op jit(solution)/shard_map/pallas_call | solution.py:33
  47.4 2.7 %collective-permute-start.2 = (f32[2,128]{1,0:T(2,128)S(1)}, f32[2,128]{1,0:T(2,128)S(1)}, u32[]{:S(2)}, u32[]{:S(2)}) collective-permute-start(f32[2,128]{1,0:T(2,128)S(1)} %get-tuple-element.65.sums), channel_id=1, source_target_pairs={{0,1},{1,0},{2,3},{3,2},{4,5},{5,4},{6,7},{7,6},{8,9},{9,8},{10,11... | collective-permute-start | bytes 3080 | tf_op jit(solution)/shard_map/ppermute | solution.py:514
  50.1 1.1 %shard_map.117.product_sums = f32[8192,128]{1,0:T(8,128)S(1)} custom-call(f32[4104,128]{1,0:T(8,128)S(1)} %get-tuple-element.67.product, f32[288,128]{1,0:T(8,128)S(1)} %get-tuple-element.50.shrink), custom_call_target="tpu_custom_call" | custom-call | tf_op jit(solution)/shard_map/pallas_call | solution.py:33
  51.2 0.2 collective-permute-done.2.other_sums
  51.4 2.7 %shard_map.118 = (f32[128,128]{1,0:T(8,128)S(1)}, f32[128,128]{1,0:T(8,128)S(1)}, f32[4104,128]{1,0:T(8,128)S(1)}, f32[8192,128]{1,0:T(8,128)S(1)}, f32[2,128,12...) custom-call(f32[2,128]{1,0:T(2,128)S(1)} %get-tuple-element.65.sums, f32[2,128]{1,0:T(2,128)S(1)} %collective-permute-done.2.other_sums, ...), custom_call_target="tpu_custom_call" | custom-call | tf_op jit(solution)/shard_map/pallas_call | solution.py:33
  54.1 1.3 %collective-permute-start.3 = (f32[2,128,128]{2,1,0:T(8,128)S(1)}, f32[2,128,128]{2,1,0:T(8,128)S(1)}, u32[]{:S(2)}, u32[]{:S(2)}) collective-permute-start(f32[2,128,128]{2,1,0:T(8,128)S(1)} %get-tuple-element.72), channel_id=1, source_target_pairs={{0,2},{2,0},{1,3},{3,1},{4,6},{6,4},{5,7},{7,5},{8,10},{10,8},{9,1... | collective-permute-start | bytes 393224 | tf_op jit(solution)/shard_map/ppermute | solution.py:514
  55.4 1.0 %shard_map.119 = (bf16[128,4096]{1,0:T(8,128)(2,1)S(1)}, bf16[128,4096]{1,0:T(8,128)(2,1)S(1)}) custom-call(f32[128,128]{1,0:T(8,128)S(1)} %get-tuple-element.73.inverse, f32[128,128]{1,0:T(8,128)S(1)} %get-tuple-element.74.slope, f32[4104,128]{1,0:T(8,128)S(1)} %get-tuple-element.75.filtered, bf16[128,4096]{1,0:T(8,128)(2,1)S(1)} %copy-done, ...), custom_call_target="tpu_custom_call" | custom-call | tf_op jit(solution)/shard_map/pallas_call | solution.py:33
  56.3 0.0 collective-permute-done.3.recv
  56.4 0.1 shard_map.120
  56.4 14.2 %all_to_all.22.totals = f32[64,2,2,128]{3,2,1,0:T(2,128)S(1)} all-to-all(f32[64,2,2,128]{3,2,1,0:T(2,128)S(1)} %shard_map.120), channel_id=1, replica_groups=mesh['x'=4,'yl'=2,'z'=8,'core'=2,'tp'=2] {'x','yl','z'}, dimensions={0} | all-to-all | bytes 262144 | tf_op jit(solution)/shard_map/all_to_all | solution.py:579
  70.6 0.2 shard_map.121
  70.8 14.4 %all_to_all.23.chip_state = f32[64,2,2,128]{3,2,1,0:T(2,128)S(1)} all-to-all(f32[64,2,2,128]{3,2,1,0:T(2,128)S(1)} %shard_map.121), channel_id=1, replica_groups=mesh['x'=4,'yl'=2,'z'=8,'core'=2,'tp'=2] {'x','yl','z'}, dimensions={0} | all-to-all | bytes 262144 | tf_op jit(solution)/shard_map/all_to_all | solution.py:581
  85.1 0.1 shard_map.122
  85.2 2.6 %collective-permute-start.4 = (f32[2,128,128]{2,1,0:T(8,128)S(1)}, f32[2,128,128]{2,1,0:T(8,128)S(1)}, u32[]{:S(2)}, u32[]{:S(2)}) collective-permute-start(f32[2,128,128]{2,1,0:T(8,128)S(1)} %get-tuple-element.82), channel_id=1, source_target_pairs={{0,2},{2,0},{1,3},{3,1},{4,6},{6,4},{5,7},{7,5},{8,10},{10,8},{9,1... | collective-permute-start | bytes 393224 | tf_op jit(solution)/shard_map/ppermute | solution.py:514
  87.8 1.2 %shard_map.123 = (f32[4104,128]{1,0:T(8,128)S(1)}, bf16[128,4096]{1,0:T(8,128)(2,1)}) custom-call(f32[4104,128]{1,0:T(8,128)S(1)} %get-tuple-element.69.grad_filtered, f32[8192,128]{1,0:T(8,128)S(1)} %get-tuple-element.70.local_adjoints, f32[288,128]{1,0:T(8,128)S(1)} %get-tuple-element.50.shrink, f32[288,128]{1,0:T(8,128)S(1)} %get-tuple-element.54.weight, ...), custom_call_target="tpu_custom_call" | custom-call | tf_op jit(solution)/shard_map/pallas_call | solution.py:33
  89.0 0.0 collective-permute-done.4.after_other
  89.1 2.7 %shard_map.124 = (bf16[128,4096]{1,0:T(8,128)(2,1)}, bf16[128,4096]{1,0:T(8,128)(2,1)}, f32[8,4096]{1,0:T(8,128)}, bf16[128,4096]{1,0:T(8,128)(2,1)}) custom-call(f32[8192,128]{1,0:T(8,128)S(1)} %get-tuple-element.70.local_adjoints, f32[288,128]{1,0:T(8,128)S(1)} %get-tuple-element.50.shrink, f32[288,128]{1,0:T(8,128)S(1)} %get-tuple-element.54.weight, ...), custom_call_target="tpu_custom_call" | custom-call | tf_op jit(solution)/shard_map/pallas_call | solution.py:33
  (2 shorter events, 0.0 us)
Async XLA Ops:
  0.6 6.4 %copy-start.1 = (bf16[128,4096]{1,0:T(8,128)(2,1)S(1)}, bf16[128,4096]{1,0:T(8,128)(2,1)}, u32[]{:S(2)}) copy-start(bf16[128,4096]{1,0:T(8,128)(2,1)} %grad.3) | copy-start | bytes 3145732
  0.6 6.4 %copy-start = (bf16[128,4096]{1,0:T(8,128)(2,1)S(1)}, bf16[128,4096]{1,0:T(8,128)(2,1)}, u32[]{:S(2)}) copy-start(bf16[128,4096]{1,0:T(8,128)(2,1)} %query.3) | copy-start | bytes 3145732
  3.7 4.3 %collective-permute-start = (f32[128,128]{1,0:T(8,128)S(1)}, f32[128,128]{1,0:T(8,128)S(1)}, u32[]{:S(2)}, u32[]{:S(2)}) collective-permute-start(f32[128,128]{1,0:T(8,128)S(1)} %get-tuple-element.57), channel_id=1, source_target_pairs={{0,2},{2,0},{1,3},{3,1},{4,6},{6,4},{5,7},{7,5},{8,10},{10,8},{9,1... | collective-permute-start | bytes 196616 | tf_op jit(solution)/shard_map/ppermute | solution.py:514
  41.7 4.1 %collective-permute-start.1 = (f32[128,128]{1,0:T(8,128)S(1)}, f32[128,128]{1,0:T(8,128)S(1)}, u32[]{:S(2)}, u32[]{:S(2)}) collective-permute-start(f32[128,128]{1,0:T(8,128)S(1)} %get-tuple-element.60), channel_id=1, source_target_pairs={{0,2},{2,0},{1,3},{3,1},{4,6},{6,4},{5,7},{7,5},{8,10},{10,8},{9,1... | collective-permute-start | bytes 196616 | tf_op jit(solution)/shard_map/ppermute | solution.py:514
  47.4 4.0 %collective-permute-start.2 = (f32[2,128]{1,0:T(2,128)S(1)}, f32[2,128]{1,0:T(2,128)S(1)}, u32[]{:S(2)}, u32[]{:S(2)}) collective-permute-start(f32[2,128]{1,0:T(2,128)S(1)} %get-tuple-element.65.sums), channel_id=1, source_target_pairs={{0,1},{1,0},{2,3},{3,2},{4,5},{5,4},{6,7},{7,6},{8,9},{9,8},{10,11... | collective-permute-start | bytes 3080 | tf_op jit(solution)/shard_map/ppermute | solution.py:514
  54.1 2.3 %collective-permute-start.3 = (f32[2,128,128]{2,1,0:T(8,128)S(1)}, f32[2,128,128]{2,1,0:T(8,128)S(1)}, u32[]{:S(2)}, u32[]{:S(2)}) collective-permute-start(f32[2,128,128]{2,1,0:T(8,128)S(1)} %get-tuple-element.72), channel_id=1, source_target_pairs={{0,2},{2,0},{1,3},{3,1},{4,6},{6,4},{5,7},{7,5},{8,10},{10,8},{9,1... | collective-permute-start | bytes 393224 | tf_op jit(solution)/shard_map/ppermute | solution.py:514
  85.2 3.9 %collective-permute-start.4 = (f32[2,128,128]{2,1,0:T(8,128)S(1)}, f32[2,128,128]{2,1,0:T(8,128)S(1)}, u32[]{:S(2)}, u32[]{:S(2)}) collective-permute-start(f32[2,128,128]{2,1,0:T(8,128)S(1)} %get-tuple-element.82), channel_id=1, source_target_pairs={{0,2},{2,0},{1,3},{3,1},{4,6},{6,4},{5,7},{7,5},{8,10},{10,8},{9,1... | collective-permute-start | bytes 393224 | tf_op jit(solution)/shard_map/ppermute | solution.py:514
